TPU v7x, 128 devices: a whole 4x4x4 slice. The times are simulated.
128 devices in a mesh: seq: 16 (over y, z), head: 8 (over x, core).
Axes of the slice: x: 4, y: 4, z: 4, core: 2. Of those that a mesh axis runs over, the one named last changes fastest.
Arguments:
- query_rows: bfloat16 [32768, 4096], P('seq', 'head'), may hold values from -6 to 6
- key_rows: bfloat16 [32768, 4096], P('seq', 'head'), may hold values from -6 to 6
- value_rows: bfloat16 [32768, 4096], P('seq', 'head'), may hold values from -6 to 6
- out_cotangent: bfloat16 [32768, 4096], P('seq', 'head'), may hold values from -6 to 6
- norm_gain: float32 [4096], P('head'), may hold values from 0.5 to 1.5
- decay_rate: float32 [32], P('head'), may hold values from 6.1035156e-06 to 0.0333333333
- document_lengths: int32 [32], replicated, may hold values from 1 to 16384, 32768 in all
- group_home: int32 [256], P('seq'), may hold values from 0 to 255, as said below
Outputs:
- query_grad: bfloat16 [32768, 4096], P('seq', 'head')
- key_grad: bfloat16 [32768, 4096], P('seq', 'head')
- value_grad: bfloat16 [32768, 4096], P('seq', 'head')
Inputs may be any that keep to these rules, and one draw needn't show every extreme that they name: document_lengths sum to 32768; the longest holds exactly half of them. group_home is a permutation of the 256 sequence groups; the groups stored on one device along seq hold exactly one group of each device's aligned block of sequence groups.
All inputs are finite; a program needn't handle non-finite values.
Results may differ from a plain program's by a relative error of at most 0.0095.
Values may be sent and summed in bfloat16 or wider, within the bound.
A program may use at most 128 MiB of HBM per device.

v0:
```python
import jax
import jax.numpy as jnp
from jax import lax
from jax.sharding import PartitionSpec as P

HEAD_SIZE = 128
SPAN = 256


EPSILON = 1e-06


def from_behind(block, axis, distance):
    devices = range(lax.axis_size(axis))
    route = [(i - distance, i) for i in devices if i - distance in devices]
    return lax.ppermute(block, axis, route)


def segment_of(positions, doc_ends):
    return jnp.sum((doc_ends <= positions[..., None]).astype(jnp.int32), axis=-1)


def span_weights(seq_spans, doc_ends, decay_rates, span_width):
    offsets = jnp.arange(span_width, dtype=jnp.int32)
    positions = seq_spans[:, None] * span_width + offsets[None, :]
    segment = segment_of(positions, doc_ends)
    before = jnp.where(seq_spans == 0, -1, segment_of(seq_spans * span_width - 1, doc_ends))
    last_segment = segment[:, -1]
    step_float = offsets.astype(jnp.float32)
    query_side = (
        jnp.exp(-decay_rates[None, None, :] * (step_float[None, :, None] + 1.0))
        * (segment == before[:, None]).astype(jnp.float32)[:, :, None]
    )
    key_side = (
        jnp.exp(-decay_rates[None, None, :] * (span_width - 1.0 - step_float)[None, :, None])
        * (segment == last_segment[:, None]).astype(jnp.float32)[:, :, None]
    )
    carry_rate = (
        jnp.exp(-decay_rates * span_width)[None, :]
        * (before == last_segment).astype(jnp.float32)[:, None]
    )
    return (query_side, key_side, carry_rate, segment)


def span_masks(segment, decay_rates, span_width):
    step_float = jnp.arange(span_width, dtype=jnp.float32)
    spread = step_float[:, None] - step_float[None, :]
    same_doc = (segment[:, :, None] == segment[:, None, :]) & (spread >= 0.0)[None]
    return jnp.where(
        same_doc[:, None],
        jnp.exp(-decay_rates[None, :, None, None] * jnp.maximum(spread, 0.0)[None, None]),
        0.0,
    )


def relay_forward(factor, state):

    def relay_turn(turn_index, incoming):
        return from_behind(
            (factor[:, None, None] * incoming + state).astype(jnp.bfloat16), "seq", 1
        ).astype(jnp.float32)

    return lax.fori_loop(0, lax.axis_size("seq") - 1, relay_turn, jnp.zeros_like(state))


def relay_backward(factor, state):

    def relay_turn(turn_index, incoming):
        return from_behind(
            (factor[:, None, None] * incoming + state).astype(jnp.bfloat16), "seq", -1
        ).astype(jnp.float32)

    return lax.fori_loop(0, lax.axis_size("seq") - 1, relay_turn, jnp.zeros_like(state))


def forward_chain(carry_rate, summary):
    span_count = carry_rate.shape[0]
    running = jnp.zeros_like(summary[0])
    factor = jnp.ones_like(carry_rate[0])
    local_prev = []
    factors = []
    for span_index in range(span_count):
        local_prev.append(running)
        factors.append(factor)
        running = carry_rate[span_index][:, None, None] * running + summary[span_index]
        factor = factor * carry_rate[span_index]
    incoming = relay_forward(factor, running)
    return jnp.stack(local_prev) + jnp.stack(factors)[:, :, None, None] * incoming[None]


def reverse_chain(carry_rate, rev_summary):
    span_count = carry_rate.shape[0]
    running = jnp.zeros_like(rev_summary[0])
    factor = jnp.ones_like(carry_rate[0])
    after_local = [running] * span_count
    after_factor = [factor] * span_count
    for span_index in range(span_count - 1, -1, -1):
        after_local[span_index] = running
        after_factor[span_index] = factor
        running = rev_summary[span_index] + carry_rate[span_index][:, None, None] * running
        factor = factor * carry_rate[span_index]
    incoming = relay_backward(factor, running)
    return jnp.stack(after_local) + jnp.stack(after_factor)[:, :, None, None] * incoming[None]


def forward_local(query_c, key_c, value_c, decay_mask, key_side):
    scores = jnp.einsum("cjhd,clhd->chjl", query_c, key_c, preferred_element_type=jnp.float32)
    mixing = (scores * decay_mask).astype(jnp.bfloat16)
    weighted = (key_side[..., None] * value_c).astype(jnp.bfloat16)
    summary = jnp.einsum("cjhd,cjhe->chde", key_c, weighted, preferred_element_type=jnp.float32)
    return (mixing, summary)


def output_local(mixing, query_c, value_c, prev_states, query_side):
    inner = jnp.einsum("chjl,clhe->cjhe", mixing, value_c, preferred_element_type=jnp.float32)
    outer = jnp.einsum("cjhd,chde->cjhe", query_c, prev_states, preferred_element_type=jnp.float32)
    return inner + query_side[..., None] * outer


def cotangent_of(attn_out, upstream, norm_gain):
    flat_out = attn_out.reshape(-1, norm_gain.shape[0])
    upstream_f = upstream.reshape(-1, norm_gain.shape[0]).astype(jnp.float32)
    squares = jnp.sum(flat_out * flat_out, axis=1)
    crossed = jnp.sum(norm_gain * upstream_f * flat_out, axis=1)
    squares, crossed = lax.psum((squares, crossed), "head")
    hidden_total = norm_gain.shape[0] * lax.axis_size("head")
    scaling = 1.0 / jnp.sqrt(squares / hidden_total + EPSILON)
    pulled = crossed / hidden_total
    grad_in = (
        scaling[:, None] * norm_gain * upstream_f
        - (scaling**3)[:, None] * flat_out * pulled[:, None]
    )
    return grad_in.astype(jnp.bfloat16).reshape(attn_out.shape)


def query_summary(query_c, grad_in, query_side):
    weighted = (query_side[..., None] * grad_in).astype(jnp.bfloat16)
    return jnp.einsum("cjhd,cjhe->chde", query_c, weighted, preferred_element_type=jnp.float32)


def backward_local(
    query_c,
    key_c,
    value_c,
    grad_in,
    mixing,
    decay_mask,
    query_side,
    key_side,
    prev_states,
    after_states,
):
    pulled = jnp.einsum("cjhe,clhe->chjl", grad_in, value_c, preferred_element_type=jnp.float32)
    score_grad = (pulled * decay_mask).astype(jnp.bfloat16)
    query_grad = jnp.einsum(
        "chjl,clhd->cjhd", score_grad, key_c, preferred_element_type=jnp.float32
    )
    query_grad = query_grad + query_side[..., None] * jnp.einsum(
        "cjhe,chde->cjhd", grad_in, prev_states, preferred_element_type=jnp.float32
    )
    key_grad = jnp.einsum(
        "chjl,cjhd->clhd", score_grad, query_c, preferred_element_type=jnp.float32
    )
    key_grad = key_grad + key_side[..., None] * jnp.einsum(
        "clhe,chde->clhd", value_c, after_states, preferred_element_type=jnp.float32
    )
    value_grad = jnp.einsum("chjl,cjhe->clhe", mixing, grad_in, preferred_element_type=jnp.float32)
    value_grad = value_grad + key_side[..., None] * jnp.einsum(
        "clhd,chde->clhe", key_c, after_states, preferred_element_type=jnp.float32
    )
    return (
        query_grad.astype(jnp.bfloat16),
        key_grad.astype(jnp.bfloat16),
        value_grad.astype(jnp.bfloat16),
    )


def shards(
    query_rows,
    key_rows,
    value_rows,
    out_cotangent,
    norm_gain,
    decay_rate,
    document_lengths,
    group_home,
):
    devices = lax.axis_size("seq")
    position = lax.axis_index("seq")
    head_count = query_rows.shape[1] // HEAD_SIZE
    group_rows = query_rows.shape[0] // devices
    span_count = query_rows.shape[0] // SPAN
    doc_ends = jnp.cumsum(document_lengths)
    target = group_home // devices
    home_slot = group_home % devices
    device_ids = jnp.arange(devices, dtype=jnp.int32)
    chosen = target[None, :] == device_ids[:, None]
    picked = jnp.sum(jnp.where(chosen, device_ids[None, :], 0), axis=1)
    sending_slot = jnp.take(home_slot, picked)
    own_spans = position * span_count + jnp.arange(span_count, dtype=jnp.int32)
    group_shape = (devices, group_rows, head_count, HEAD_SIZE)
    span_shape = (span_count, SPAN, head_count, HEAD_SIZE)

    def outgoing(rows):
        return jnp.take(rows.reshape(group_shape), picked, axis=0)

    arrived = (
        lax.all_to_all(outgoing(query_rows), "seq", split_axis=0, concat_axis=0, tiled=True),
        lax.all_to_all(outgoing(key_rows), "seq", split_axis=0, concat_axis=0, tiled=True),
        lax.all_to_all(outgoing(value_rows), "seq", split_axis=0, concat_axis=0, tiled=True),
        lax.all_to_all(outgoing(out_cotangent), "seq", split_axis=0, concat_axis=0, tiled=True),
        lax.all_to_all(sending_slot, "seq", split_axis=0, concat_axis=0, tiled=True),
    )
    arrived_slot = arrived[4]
    matches = arrived_slot[None, :] == device_ids[:, None]
    source_pick = jnp.sum(jnp.where(matches, device_ids[None, :], 0), axis=1)

    def ordered(groups):
        return jnp.take(groups, source_pick, axis=0).reshape(span_shape)

    query_s = ordered(arrived[0])
    key_s = ordered(arrived[1])
    value_s = ordered(arrived[2])
    query_side, key_side, carry_rate, segment = span_weights(own_spans, doc_ends, decay_rate, SPAN)
    decay_mask = span_masks(segment, decay_rate, SPAN)
    mixing, summary = forward_local(query_s, key_s, value_s, decay_mask, key_side)
    upstream_s = ordered(arrived[3])
    prev_states = forward_chain(carry_rate, summary).astype(jnp.bfloat16)
    attn_out = output_local(mixing, query_s, value_s, prev_states, query_side)
    grad_in = cotangent_of(attn_out, upstream_s, norm_gain)
    rev_summary = query_summary(query_s, grad_in, query_side)
    after_states = reverse_chain(carry_rate, rev_summary).astype(jnp.bfloat16)
    query_grad, key_grad, value_grad = backward_local(
        query_s,
        key_s,
        value_s,
        grad_in,
        mixing,
        decay_mask,
        query_side,
        key_side,
        prev_states,
        after_states,
    )

    def homeward(values):
        return jnp.take(values.reshape(group_shape), arrived_slot, axis=0)

    returned = (
        lax.all_to_all(homeward(query_grad), "seq", split_axis=0, concat_axis=0, tiled=True),
        lax.all_to_all(homeward(key_grad), "seq", split_axis=0, concat_axis=0, tiled=True),
        lax.all_to_all(homeward(value_grad), "seq", split_axis=0, concat_axis=0, tiled=True),
    )
    flat_shape = query_rows.shape
    return tuple((jnp.take(piece, target, axis=0).reshape(flat_shape) for piece in returned))


def solution(mesh):
    in_specs = (
        P("seq", "head"),
        P("seq", "head"),
        P("seq", "head"),
        P("seq", "head"),
        P("head"),
        P("head"),
        P(),
        P("seq"),
    )
    out_specs = (P("seq", "head"), P("seq", "head"), P("seq", "head"))
    return jax.shard_map(shards, mesh=mesh, in_specs=in_specs, out_specs=out_specs, check_vma=False)
```

profile of v0, /device:TPU:0, one launch (start us, length us, event | category | flops | bytes accessed | tf_op | source)
XLA Modules:
  0.0 705.3 jit_solution(379513629993014268)
XLA Ops:
  3.5 8.1 %all-to-all-start.1 = ((s32[16,1,1]{2,1,0:T(1,128)}), s32[16,1,1]{2,1,0:T(1,128)S(1)}, u32[]{:S(2)}, u32[]{:S(2)}) async-start(s32[16,1,1]{2,1,0:T(1,128)} %copy.316), calls=%async_computation.1 | async-start | bytes 16384 | tf_op jit(solution)/shard_map/all_to_all | solution.py:212
  23.1 3.7 gather_fusion.3
  26.8 4.0 reshape.562
  34.2 3.7 gather_fusion.5
  37.9 4.0 reshape.560
  49.1 6.5 broadcast_select_fusion.9
  55.6 35.0 %all_to_all.41 = bf16[16,128,4,128]{3,1,2,0:T(8,128)(2,1)S(1)} all-to-all(bf16[16,128,4,128]{3,1,2,0:T(8,128)(2,1)} %get-tuple-element.179), channel_id=1, replica_groups=mesh['seq'=16,'head'=8] {'seq'}, dimensions={0} | all-to-all | bytes 4194304 | tf_op jit(solution)/shard_map/all_to_all | solution.py:211
  90.6 4.6 all-to-all-start.2
  97.0 26.0 %all-to-all-done.2 = bf16[16,128,4,128]{3,1,2,0:T(8,128)(2,1)} async-done(((bf16[16,128,4,128]{3,1,2,0:T(8,128)(2,1)}), bf16[16,128,4,128]{3,1,2,0:T(8,128)(2,1)}, u32[]{:S(2)}, u32[]{:S(2)}) %all-to-all-start.2) | async-done | bytes 2097184 | tf_op jit(solution)/shard_map/all_to_all | solution.py:210
  123.0 4.6 all-to-all-start.3
  127.9 27.3 %all-to-all-done.3 = bf16[16,128,4,128]{3,1,2,0:T(8,128)(2,1)} async-done(((bf16[16,128,4,128]{3,1,2,0:T(8,128)(2,1)}), bf16[16,128,4,128]{3,1,2,0:T(8,128)(2,1)}, u32[]{:S(2)}, u32[]{:S(2)}) %all-to-all-start.3) | async-done | bytes 2097184 | tf_op jit(solution)/shard_map/all_to_all | solution.py:208
  155.2 4.6 all-to-all-start
  172.6 14.9 %all-to-all-done = bf16[16,128,4,128]{3,1,2,0:T(8,128)(2,1)} async-done(((bf16[16,128,4,128]{3,1,2,0:T(8,128)(2,1)}), bf16[16,128,4,128]{3,1,2,0:T(8,128)(2,1)}, u32[]{:S(2)}, u32[]{:S(2)}) %all-to-all-start) | async-done | bytes 2097184 | tf_op jit(solution)/shard_map/all_to_all | solution.py:209
  187.5 3.7 gather_fusion.2
  191.3 5.8 select_convert_fusion
  199.4 5.5 copy.339
  224.0 125.0 %while.22 = (s32[]{:T(128)}, f32[4,128,128]{2,1,0:T(8,128)S(1)}, f32[4]{0:T(128)S(1)}, f32[4,128,128]{2,1,0:T(8,128)S(1)}, s32[]{:T(128)}, /*index=5*/s32[]{:T(128)}) while((s32[]{:T(128)}, f32[4,128,128]{2,1,0:T(8,128)S(1)}, f32[4]{0:T(128)S(1)}, f32[4,128,128]{2,1,0:T(8,128)S(1)}, s32[]{:T(128)}, /*index=5*/s32[]{:T(128)}) %tuple.104), condition=%wide.region_6.8_spmd.clone, body=%wide.region_5.7_spmd.clone.sunk | while | flops 327683 | bytes 1572999 | solution.py:63
  230.2 4.4 collective-permute-start
  237.5 4.4 collective-permute-start
  244.6 4.4 collective-permute-start
  251.6 4.4 collective-permute-start
  258.6 4.4 collective-permute-start
  265.9 6.2 collective-permute-start
  274.7 6.2 collective-permute-start
  283.6 6.5 collective-permute-start
  292.8 6.5 collective-permute-start
  301.9 6.5 collective-permute-start
  311.0 6.7 collective-permute-start
  321.4 7.1 %collective-permute-start = (bf16[4,128,128]{2,1,0:T(8,128)(2,1)S(1)}, bf16[4,128,128]{2,1,0:T(8,128)(2,1)S(1)}, u32[]{:S(2)}, u32[]{:S(2)}) collective-permute-start(bf16[4,128,128]{2,1,0:T(8,128)(2,1)S(1)} %fusion.70), channel_id=1, source_target_pairs={{0,8},{8,16},{16,24},{24,32},{32,40},{40,48},{48,56},{56,64},{64,7... | collective-permute-start | bytes 393224 | tf_op jit(solution)/shard_map/while/body/eval_jaxpr/ppermute | solution.py:16
  331.6 6.2 collective-permute-start
  340.4 6.0 collective-permute-start
  349.0 7.6 %multiply_reduce_fusion.1 = (f32[8,256]{1,0:T(8,128)S(1)}, f32[8,256]{1,0:T(8,128)S(1)}, f32[8,256,4,128]{1,3,2,0:T(8,128)}) fusion(f32[8,256,4,128]{1,3,2,0:T(8,128)} %copy.339, f32[4,128]{1,0:T(4,128)S(1)} %bitcast.238, bf16[8,256,4,128]{3,1,0,2:T(8,128)(2,1)S(1)} %bitcast.220, f32[8,4,128,128]{3,2,1,0:T(8,128)} %copy-done.10, ...), kind=kOutput, calls=%fused_computation.39 | convolution fusion | flops 277344256 | bytes 17090688 | tf_op jit(solution)/shard_map/cjhd,chde->cjhe/dot_general | solution.py:116
  356.6 23.8 %all-reduce = (f32[2048]{0:T(1024)S(1)}, f32[2048]{0:T(1024)S(1)}) all-reduce(f32[2048]{0:T(1024)S(1)} %bitcast.236, f32[2048]{0:T(1024)S(1)} %bitcast.237), channel_id=1, replica_groups=mesh['seq'=16,'head'=8] {'head'}, use_global_device_ids=true, to_apply=%region_10.12 | all-reduce | flops 4096 | bytes 32768 | tf_op jit(solution)/shard_map/psum | solution.py:125
  380.5 4.8 subtract_convert_fusion
  400.1 142.4 %while.23 = (s32[]{:T(128)}, f32[4,128,128]{2,1,0:T(8,128)S(1)}, f32[4]{0:T(128)S(1)}, f32[4,128,128]{2,1,0:T(8,128)S(1)}, s32[]{:T(128)}, /*index=5*/s32[]{:T(128)}) while((s32[]{:T(128)}, f32[4,128,128]{2,1,0:T(8,128)S(1)}, f32[4]{0:T(128)S(1)}, f32[4,128,128]{2,1,0:T(8,128)S(1)}, s32[]{:T(128)}, /*index=5*/s32[]{:T(128)}) %tuple.107), condition=%wide.region_12.14_spmd.clone, body=%wide.region_11.13_spmd.clone.sunk | while | flops 327683 | bytes 1572999 | solution.py:73
  401.5 8.1 %collective-permute-done.1 = bf16[4,128,128]{2,1,0:T(8,128)(2,1)S(1)} collective-permute-done((bf16[4,128,128]{2,1,0:T(8,128)(2,1)S(1)}, bf16[4,128,128]{2,1,0:T(8,128)(2,1)S(1)}, u32[]{:S(2)}, u32[]{:S(2)}) %collective-permute-start.1) | collective-permute-done | bytes 131104 | tf_op jit(solution)/shard_map/while/body/eval_jaxpr/ppermute | solution.py:16
  411.0 8.1 %collective-permute-done.1 = bf16[4,128,128]{2,1,0:T(8,128)(2,1)S(1)} collective-permute-done((bf16[4,128,128]{2,1,0:T(8,128)(2,1)S(1)}, bf16[4,128,128]{2,1,0:T(8,128)(2,1)S(1)}, u32[]{:S(2)}, u32[]{:S(2)}) %collective-permute-start.1) | collective-permute-done | bytes 131104 | tf_op jit(solution)/shard_map/while/body/eval_jaxpr/ppermute | solution.py:16
  420.6 8.1 %collective-permute-done.1 = bf16[4,128,128]{2,1,0:T(8,128)(2,1)S(1)} collective-permute-done((bf16[4,128,128]{2,1,0:T(8,128)(2,1)S(1)}, bf16[4,128,128]{2,1,0:T(8,128)(2,1)S(1)}, u32[]{:S(2)}, u32[]{:S(2)}) %collective-permute-start.1) | collective-permute-done | bytes 131104 | tf_op jit(solution)/shard_map/while/body/eval_jaxpr/ppermute | solution.py:16
  430.1 8.1 %collective-permute-done.1 = bf16[4,128,128]{2,1,0:T(8,128)(2,1)S(1)} collective-permute-done((bf16[4,128,128]{2,1,0:T(8,128)(2,1)S(1)}, bf16[4,128,128]{2,1,0:T(8,128)(2,1)S(1)}, u32[]{:S(2)}, u32[]{:S(2)}) %collective-permute-start.1) | collective-permute-done | bytes 131104 | tf_op jit(solution)/shard_map/while/body/eval_jaxpr/ppermute | solution.py:16
  439.7 8.6 %collective-permute-done.1 = bf16[4,128,128]{2,1,0:T(8,128)(2,1)S(1)} collective-permute-done((bf16[4,128,128]{2,1,0:T(8,128)(2,1)S(1)}, bf16[4,128,128]{2,1,0:T(8,128)(2,1)S(1)}, u32[]{:S(2)}, u32[]{:S(2)}) %collective-permute-start.1) | collective-permute-done | bytes 131104 | tf_op jit(solution)/shard_map/while/body/eval_jaxpr/ppermute | solution.py:16
  449.7 9.1 %collective-permute-done.1 = bf16[4,128,128]{2,1,0:T(8,128)(2,1)S(1)} collective-permute-done((bf16[4,128,128]{2,1,0:T(8,128)(2,1)S(1)}, bf16[4,128,128]{2,1,0:T(8,128)(2,1)S(1)}, u32[]{:S(2)}, u32[]{:S(2)}) %collective-permute-start.1) | collective-permute-done | bytes 131104 | tf_op jit(solution)/shard_map/while/body/eval_jaxpr/ppermute | solution.py:16
  460.3 8.2 %collective-permute-done.1 = bf16[4,128,128]{2,1,0:T(8,128)(2,1)S(1)} collective-permute-done((bf16[4,128,128]{2,1,0:T(8,128)(2,1)S(1)}, bf16[4,128,128]{2,1,0:T(8,128)(2,1)S(1)}, u32[]{:S(2)}, u32[]{:S(2)}) %collective-permute-start.1) | collective-permute-done | bytes 131104 | tf_op jit(solution)/shard_map/while/body/eval_jaxpr/ppermute | solution.py:16
  469.9 7.0 collective-permute-done.1
  478.3 7.4 %collective-permute-done.1 = bf16[4,128,128]{2,1,0:T(8,128)(2,1)S(1)} collective-permute-done((bf16[4,128,128]{2,1,0:T(8,128)(2,1)S(1)}, bf16[4,128,128]{2,1,0:T(8,128)(2,1)S(1)}, u32[]{:S(2)}, u32[]{:S(2)}) %collective-permute-start.1) | collective-permute-done | bytes 131104 | tf_op jit(solution)/shard_map/while/body/eval_jaxpr/ppermute | solution.py:16
  487.2 7.7 %collective-permute-done.1 = bf16[4,128,128]{2,1,0:T(8,128)(2,1)S(1)} collective-permute-done((bf16[4,128,128]{2,1,0:T(8,128)(2,1)S(1)}, bf16[4,128,128]{2,1,0:T(8,128)(2,1)S(1)}, u32[]{:S(2)}, u32[]{:S(2)}) %collective-permute-start.1) | collective-permute-done | bytes 131104 | tf_op jit(solution)/shard_map/while/body/eval_jaxpr/ppermute | solution.py:16
  496.3 7.7 %collective-permute-done.1 = bf16[4,128,128]{2,1,0:T(8,128)(2,1)S(1)} collective-permute-done((bf16[4,128,128]{2,1,0:T(8,128)(2,1)S(1)}, bf16[4,128,128]{2,1,0:T(8,128)(2,1)S(1)}, u32[]{:S(2)}, u32[]{:S(2)}) %collective-permute-start.1) | collective-permute-done | bytes 131104 | tf_op jit(solution)/shard_map/while/body/eval_jaxpr/ppermute | solution.py:16
  505.4 8.0 %collective-permute-done.1 = bf16[4,128,128]{2,1,0:T(8,128)(2,1)S(1)} collective-permute-done((bf16[4,128,128]{2,1,0:T(8,128)(2,1)S(1)}, bf16[4,128,128]{2,1,0:T(8,128)(2,1)S(1)}, u32[]{:S(2)}, u32[]{:S(2)}) %collective-permute-start.1) | collective-permute-done | bytes 131104 | tf_op jit(solution)/shard_map/while/body/eval_jaxpr/ppermute | solution.py:16
  514.9 9.2 %collective-permute-done.1 = bf16[4,128,128]{2,1,0:T(8,128)(2,1)S(1)} collective-permute-done((bf16[4,128,128]{2,1,0:T(8,128)(2,1)S(1)}, bf16[4,128,128]{2,1,0:T(8,128)(2,1)S(1)}, u32[]{:S(2)}, u32[]{:S(2)}) %collective-permute-start.1) | collective-permute-done | bytes 131104 | tf_op jit(solution)/shard_map/while/body/eval_jaxpr/ppermute | solution.py:16
  525.6 7.7 %collective-permute-done.1 = bf16[4,128,128]{2,1,0:T(8,128)(2,1)S(1)} collective-permute-done((bf16[4,128,128]{2,1,0:T(8,128)(2,1)S(1)}, bf16[4,128,128]{2,1,0:T(8,128)(2,1)S(1)}, u32[]{:S(2)}, u32[]{:S(2)}) %collective-permute-start.1) | collective-permute-done | bytes 131104 | tf_op jit(solution)/shard_map/while/body/eval_jaxpr/ppermute | solution.py:16
  534.7 7.7 %collective-permute-done.1 = bf16[4,128,128]{2,1,0:T(8,128)(2,1)S(1)} collective-permute-done((bf16[4,128,128]{2,1,0:T(8,128)(2,1)S(1)}, bf16[4,128,128]{2,1,0:T(8,128)(2,1)S(1)}, u32[]{:S(2)}, u32[]{:S(2)}) %collective-permute-start.1) | collective-permute-done | bytes 131104 | tf_op jit(solution)/shard_map/while/body/eval_jaxpr/ppermute | solution.py:16
  542.5 5.8 fusion.7
  548.2 3.9 copy.355
  552.1 5.6 fusion.9
  557.8 3.9 copy.351
  569.1 5.0 fusion.11
  574.1 4.1 copy.345
  578.2 3.9 gather_fusion.9
  582.1 4.2 broadcast_select_fusion.3
  586.3 42.8 %all_to_all.42 = bf16[16,128,4,128]{3,1,2,0:T(8,128)(2,1)} all-to-all(bf16[16,128,4,128]{3,1,2,0:T(8,128)(2,1)S(1)} %get-tuple-element.172), channel_id=1, replica_groups=mesh['seq'=16,'head'=8] {'seq'}, dimensions={0} | all-to-all | bytes 4194304 | tf_op jit(solution)/shard_map/all_to_all | solution.py:252
  629.1 34.9 %all_to_all.43 = bf16[16,128,4,128]{3,1,2,0:T(8,128)(2,1)} all-to-all(bf16[16,128,4,128]{3,1,2,0:T(8,128)(2,1)S(1)} %get-tuple-element.173), channel_id=1, replica_groups=mesh['seq'=16,'head'=8] {'seq'}, dimensions={0} | all-to-all | bytes 4194304 | tf_op jit(solution)/shard_map/all_to_all | solution.py:251
  663.9 4.4 all-to-all-start.5
  670.9 3.7 gather_fusion.12
  674.7 13.2 %all-to-all-done.5 = bf16[16,128,4,128]{3,1,2,0:T(8,128)(2,1)} async-done(((bf16[16,128,4,128]{3,1,2,0:T(8,128)(2,1)}), bf16[16,128,4,128]{3,1,2,0:T(8,128)(2,1)}, u32[]{:S(2)}, u32[]{:S(2)}) %all-to-all-start.5) | async-done | bytes 2097184 | tf_op jit(solution)/shard_map/all_to_all | solution.py:250
  687.9 3.7 gather_fusion.10
  (248 shorter events, 164.8 us)
Async XLA Ops:
  3.5 52.1 %all-to-all-start.1 = ((s32[16,1,1]{2,1,0:T(1,128)}), s32[16,1,1]{2,1,0:T(1,128)S(1)}, u32[]{:S(2)}, u32[]{:S(2)}) async-start(s32[16,1,1]{2,1,0:T(1,128)} %copy.316), calls=%async_computation.1 | async-start | bytes 16384 | tf_op jit(solution)/shard_map/all_to_all | solution.py:212
  90.6 4.6 copy-start.21
  90.6 32.4 %all-to-all-start.2 = ((bf16[16,128,4,128]{3,1,2,0:T(8,128)(2,1)}), bf16[16,128,4,128]{3,1,2,0:T(8,128)(2,1)}, u32[]{:S(2)}, u32[]{:S(2)}) async-start(bf16[16,128,4,128]{3,1,2,0:T(8,128)(2,1)} %get-tuple-element.180), calls=%async_computation.2 | async-start | bytes 4194304 | tf_op jit(solution)/shard_map/all_to_all | solution.py:210
  123.0 4.7 copy-start.22
  123.0 32.3 %all-to-all-start.3 = ((bf16[16,128,4,128]{3,1,2,0:T(8,128)(2,1)}), bf16[16,128,4,128]{3,1,2,0:T(8,128)(2,1)}, u32[]{:S(2)}, u32[]{:S(2)}) async-start(bf16[16,128,4,128]{3,1,2,0:T(8,128)(2,1)} %get-tuple-element.181), calls=%async_computation.3 | async-start | bytes 4194304 | tf_op jit(solution)/shard_map/all_to_all | solution.py:208
  155.2 32.3 %all-to-all-start = ((bf16[16,128,4,128]{3,1,2,0:T(8,128)(2,1)}), bf16[16,128,4,128]{3,1,2,0:T(8,128)(2,1)}, u32[]{:S(2)}, u32[]{:S(2)}) async-start(bf16[16,128,4,128]{3,1,2,0:T(8,128)(2,1)} %get-tuple-element.182), calls=%async_computation | async-start | bytes 4194304 | tf_op jit(solution)/shard_map/all_to_all | solution.py:209
  172.6 18.7 %copy-start.13 = (bf16[16,128,4,128]{3,1,2,0:T(8,128)(2,1)S(1)}, bf16[16,128,4,128]{3,1,2,0:T(8,128)(2,1)}, u32[]{:S(2)}) copy-start(bf16[16,128,4,128]{3,1,2,0:T(8,128)(2,1)} %gather_fusion.8) | copy-start | bytes 6291460
  199.4 5.5 copy-start.15
  204.9 2.3 copy-start.14
  211.5 6.7 copy-start
  214.1 1.3 copy-start.2
  214.2 2.4 copy-start.4
  214.2 2.6 copy-start.16
  214.2 2.7 copy-start.18
  218.2 3.5 copy-start.7
  218.2 3.5 copy-start.9
  222.3 126.6 %copy-start.5 = (bf16[16,128,4,128]{3,1,0,2:T(8,128)(2,1)S(1)}, bf16[16,128,4,128]{3,1,0,2:T(8,128)(2,1)}, u32[]{:S(2)}) copy-start(bf16[16,128,4,128]{3,1,0,2:T(8,128)(2,1)} %copy.325) | copy-start | bytes 6291460
  222.7 1.3 copy-start.10
  224.0 125.0 %copy-start.20 = (f32[512]{0:T(512)S(1)}, f32[512]{0:T(512)}, u32[]{:S(2)}) copy-start(f32[512]{0:T(512)} %param.18) | copy-start | bytes 6148
  224.1 6.0 collective-permute-start
  230.2 7.1 %collective-permute-start = (bf16[4,128,128]{2,1,0:T(8,128)(2,1)S(1)}, bf16[4,128,128]{2,1,0:T(8,128)(2,1)S(1)}, u32[]{:S(2)}, u32[]{:S(2)}) collective-permute-start(bf16[4,128,128]{2,1,0:T(8,128)(2,1)S(1)} %fusion.70), channel_id=1, source_target_pairs={{0,8},{8,16},{16,24},{24,32},{32,40},{40,48},{48,56},{56,64},{64,7... | collective-permute-start | bytes 393224 | tf_op jit(solution)/shard_map/while/body/eval_jaxpr/ppermute | solution.py:16
  237.5 6.9 collective-permute-start
  244.6 6.9 collective-permute-start
  251.6 6.9 collective-permute-start
  258.6 7.1 %collective-permute-start = (bf16[4,128,128]{2,1,0:T(8,128)(2,1)S(1)}, bf16[4,128,128]{2,1,0:T(8,128)(2,1)S(1)}, u32[]{:S(2)}, u32[]{:S(2)}) collective-permute-start(bf16[4,128,128]{2,1,0:T(8,128)(2,1)S(1)} %fusion.70), channel_id=1, source_target_pairs={{0,8},{8,16},{16,24},{24,32},{32,40},{40,48},{48,56},{56,64},{64,7... | collective-permute-start | bytes 393224 | tf_op jit(solution)/shard_map/while/body/eval_jaxpr/ppermute | solution.py:16
  265.9 8.7 %collective-permute-start = (bf16[4,128,128]{2,1,0:T(8,128)(2,1)S(1)}, bf16[4,128,128]{2,1,0:T(8,128)(2,1)S(1)}, u32[]{:S(2)}, u32[]{:S(2)}) collective-permute-start(bf16[4,128,128]{2,1,0:T(8,128)(2,1)S(1)} %fusion.70), channel_id=1, source_target_pairs={{0,8},{8,16},{16,24},{24,32},{32,40},{40,48},{48,56},{56,64},{64,7... | collective-permute-start | bytes 393224 | tf_op jit(solution)/shard_map/while/body/eval_jaxpr/ppermute | solution.py:16
  274.7 8.7 %collective-permute-start = (bf16[4,128,128]{2,1,0:T(8,128)(2,1)S(1)}, bf16[4,128,128]{2,1,0:T(8,128)(2,1)S(1)}, u32[]{:S(2)}, u32[]{:S(2)}) collective-permute-start(bf16[4,128,128]{2,1,0:T(8,128)(2,1)S(1)} %fusion.70), channel_id=1, source_target_pairs={{0,8},{8,16},{16,24},{24,32},{32,40},{40,48},{48,56},{56,64},{64,7... | collective-permute-start | bytes 393224 | tf_op jit(solution)/shard_map/while/body/eval_jaxpr/ppermute | solution.py:16
  283.6 9.0 %collective-permute-start = (bf16[4,128,128]{2,1,0:T(8,128)(2,1)S(1)}, bf16[4,128,128]{2,1,0:T(8,128)(2,1)S(1)}, u32[]{:S(2)}, u32[]{:S(2)}) collective-permute-start(bf16[4,128,128]{2,1,0:T(8,128)(2,1)S(1)} %fusion.70), channel_id=1, source_target_pairs={{0,8},{8,16},{16,24},{24,32},{32,40},{40,48},{48,56},{56,64},{64,7... | collective-permute-start | bytes 393224 | tf_op jit(solution)/shard_map/while/body/eval_jaxpr/ppermute | solution.py:16
  292.8 9.0 %collective-permute-start = (bf16[4,128,128]{2,1,0:T(8,128)(2,1)S(1)}, bf16[4,128,128]{2,1,0:T(8,128)(2,1)S(1)}, u32[]{:S(2)}, u32[]{:S(2)}) collective-permute-start(bf16[4,128,128]{2,1,0:T(8,128)(2,1)S(1)} %fusion.70), channel_id=1, source_target_pairs={{0,8},{8,16},{16,24},{24,32},{32,40},{40,48},{48,56},{56,64},{64,7... | collective-permute-start | bytes 393224 | tf_op jit(solution)/shard_map/while/body/eval_jaxpr/ppermute | solution.py:16
  301.9 9.0 %collective-permute-start = (bf16[4,128,128]{2,1,0:T(8,128)(2,1)S(1)}, bf16[4,128,128]{2,1,0:T(8,128)(2,1)S(1)}, u32[]{:S(2)}, u32[]{:S(2)}) collective-permute-start(bf16[4,128,128]{2,1,0:T(8,128)(2,1)S(1)} %fusion.70), channel_id=1, source_target_pairs={{0,8},{8,16},{16,24},{24,32},{32,40},{40,48},{48,56},{56,64},{64,7... | collective-permute-start | bytes 393224 | tf_op jit(solution)/shard_map/while/body/eval_jaxpr/ppermute | solution.py:16
  311.0 10.3 %collective-permute-start = (bf16[4,128,128]{2,1,0:T(8,128)(2,1)S(1)}, bf16[4,128,128]{2,1,0:T(8,128)(2,1)S(1)}, u32[]{:S(2)}, u32[]{:S(2)}) collective-permute-start(bf16[4,128,128]{2,1,0:T(8,128)(2,1)S(1)} %fusion.70), channel_id=1, source_target_pairs={{0,8},{8,16},{16,24},{24,32},{32,40},{40,48},{48,56},{56,64},{64,7... | collective-permute-start | bytes 393224 | tf_op jit(solution)/shard_map/while/body/eval_jaxpr/ppermute | solution.py:16
  321.4 10.0 %collective-permute-start = (bf16[4,128,128]{2,1,0:T(8,128)(2,1)S(1)}, bf16[4,128,128]{2,1,0:T(8,128)(2,1)S(1)}, u32[]{:S(2)}, u32[]{:S(2)}) collective-permute-start(bf16[4,128,128]{2,1,0:T(8,128)(2,1)S(1)} %fusion.70), channel_id=1, source_target_pairs={{0,8},{8,16},{16,24},{24,32},{32,40},{40,48},{48,56},{56,64},{64,7... | collective-permute-start | bytes 393224 | tf_op jit(solution)/shard_map/while/body/eval_jaxpr/ppermute | solution.py:16
  331.6 8.7 %collective-permute-start = (bf16[4,128,128]{2,1,0:T(8,128)(2,1)S(1)}, bf16[4,128,128]{2,1,0:T(8,128)(2,1)S(1)}, u32[]{:S(2)}, u32[]{:S(2)}) collective-permute-start(bf16[4,128,128]{2,1,0:T(8,128)(2,1)S(1)} %fusion.70), channel_id=1, source_target_pairs={{0,8},{8,16},{16,24},{24,32},{32,40},{40,48},{48,56},{56,64},{64,7... | collective-permute-start | bytes 393224 | tf_op jit(solution)/shard_map/while/body/eval_jaxpr/ppermute | solution.py:16
  340.4 8.5 %collective-permute-start = (bf16[4,128,128]{2,1,0:T(8,128)(2,1)S(1)}, bf16[4,128,128]{2,1,0:T(8,128)(2,1)S(1)}, u32[]{:S(2)}, u32[]{:S(2)}) collective-permute-start(bf16[4,128,128]{2,1,0:T(8,128)(2,1)S(1)} %fusion.70), channel_id=1, source_target_pairs={{0,8},{8,16},{16,24},{24,32},{32,40},{40,48},{48,56},{56,64},{64,7... | collective-permute-start | bytes 393224 | tf_op jit(solution)/shard_map/while/body/eval_jaxpr/ppermute | solution.py:16
  380.4 4.8 copy-start.8
  385.3 2.7 copy-start.6
  388.0 1.6 copy-start.1
  388.0 1.9 copy-start.17
  388.0 2.0 copy-start.19
  391.8 2.9 copy-start.3
  398.7 1.3 copy-start.11
  400.2 9.4 %collective-permute-start.1 = (bf16[4,128,128]{2,1,0:T(8,128)(2,1)S(1)}, bf16[4,128,128]{2,1,0:T(8,128)(2,1)S(1)}, u32[]{:S(2)}, u32[]{:S(2)}) collective-permute-start(bf16[4,128,128]{2,1,0:T(8,128)(2,1)S(1)} %fusion.71), channel_id=1, source_target_pairs={{8,0},{16,8},{24,16},{32,24},{40,32},{48,40},{56,48},{64,56},{72,6... | collective-permute-start | bytes 393224 | tf_op jit(solution)/shard_map/while/body/eval_jaxpr/ppermute | solution.py:16
  409.7 9.4 %collective-permute-start.1 = (bf16[4,128,128]{2,1,0:T(8,128)(2,1)S(1)}, bf16[4,128,128]{2,1,0:T(8,128)(2,1)S(1)}, u32[]{:S(2)}, u32[]{:S(2)}) collective-permute-start(bf16[4,128,128]{2,1,0:T(8,128)(2,1)S(1)} %fusion.71), channel_id=1, source_target_pairs={{8,0},{16,8},{24,16},{32,24},{40,32},{48,40},{56,48},{64,56},{72,6... | collective-permute-start | bytes 393224 | tf_op jit(solution)/shard_map/while/body/eval_jaxpr/ppermute | solution.py:16
  419.3 9.4 %collective-permute-start.1 = (bf16[4,128,128]{2,1,0:T(8,128)(2,1)S(1)}, bf16[4,128,128]{2,1,0:T(8,128)(2,1)S(1)}, u32[]{:S(2)}, u32[]{:S(2)}) collective-permute-start(bf16[4,128,128]{2,1,0:T(8,128)(2,1)S(1)} %fusion.71), channel_id=1, source_target_pairs={{8,0},{16,8},{24,16},{32,24},{40,32},{48,40},{56,48},{64,56},{72,6... | collective-permute-start | bytes 393224 | tf_op jit(solution)/shard_map/while/body/eval_jaxpr/ppermute | solution.py:16
  428.8 9.4 %collective-permute-start.1 = (bf16[4,128,128]{2,1,0:T(8,128)(2,1)S(1)}, bf16[4,128,128]{2,1,0:T(8,128)(2,1)S(1)}, u32[]{:S(2)}, u32[]{:S(2)}) collective-permute-start(bf16[4,128,128]{2,1,0:T(8,128)(2,1)S(1)} %fusion.71), channel_id=1, source_target_pairs={{8,0},{16,8},{24,16},{32,24},{40,32},{48,40},{56,48},{64,56},{72,6... | collective-permute-start | bytes 393224 | tf_op jit(solution)/shard_map/while/body/eval_jaxpr/ppermute | solution.py:16
  438.4 9.9 %collective-permute-start.1 = (bf16[4,128,128]{2,1,0:T(8,128)(2,1)S(1)}, bf16[4,128,128]{2,1,0:T(8,128)(2,1)S(1)}, u32[]{:S(2)}, u32[]{:S(2)}) collective-permute-start(bf16[4,128,128]{2,1,0:T(8,128)(2,1)S(1)} %fusion.71), channel_id=1, source_target_pairs={{8,0},{16,8},{24,16},{32,24},{40,32},{48,40},{56,48},{64,56},{72,6... | collective-permute-start | bytes 393224 | tf_op jit(solution)/shard_map/while/body/eval_jaxpr/ppermute | solution.py:16
  448.4 10.4 %collective-permute-start.1 = (bf16[4,128,128]{2,1,0:T(8,128)(2,1)S(1)}, bf16[4,128,128]{2,1,0:T(8,128)(2,1)S(1)}, u32[]{:S(2)}, u32[]{:S(2)}) collective-permute-start(bf16[4,128,128]{2,1,0:T(8,128)(2,1)S(1)} %fusion.71), channel_id=1, source_target_pairs={{8,0},{16,8},{24,16},{32,24},{40,32},{48,40},{56,48},{64,56},{72,6... | collective-permute-start | bytes 393224 | tf_op jit(solution)/shard_map/while/body/eval_jaxpr/ppermute | solution.py:16
  459.0 9.5 %collective-permute-start.1 = (bf16[4,128,128]{2,1,0:T(8,128)(2,1)S(1)}, bf16[4,128,128]{2,1,0:T(8,128)(2,1)S(1)}, u32[]{:S(2)}, u32[]{:S(2)}) collective-permute-start(bf16[4,128,128]{2,1,0:T(8,128)(2,1)S(1)} %fusion.71), channel_id=1, source_target_pairs={{8,0},{16,8},{24,16},{32,24},{40,32},{48,40},{56,48},{64,56},{72,6... | collective-permute-start | bytes 393224 | tf_op jit(solution)/shard_map/while/body/eval_jaxpr/ppermute | solution.py:16
  468.6 8.3 %collective-permute-start.1 = (bf16[4,128,128]{2,1,0:T(8,128)(2,1)S(1)}, bf16[4,128,128]{2,1,0:T(8,128)(2,1)S(1)}, u32[]{:S(2)}, u32[]{:S(2)}) collective-permute-start(bf16[4,128,128]{2,1,0:T(8,128)(2,1)S(1)} %fusion.71), channel_id=1, source_target_pairs={{8,0},{16,8},{24,16},{32,24},{40,32},{48,40},{56,48},{64,56},{72,6... | collective-permute-start | bytes 393224 | tf_op jit(solution)/shard_map/while/body/eval_jaxpr/ppermute | solution.py:16
  477.0 8.7 %collective-permute-start.1 = (bf16[4,128,128]{2,1,0:T(8,128)(2,1)S(1)}, bf16[4,128,128]{2,1,0:T(8,128)(2,1)S(1)}, u32[]{:S(2)}, u32[]{:S(2)}) collective-permute-start(bf16[4,128,128]{2,1,0:T(8,128)(2,1)S(1)} %fusion.71), channel_id=1, source_target_pairs={{8,0},{16,8},{24,16},{32,24},{40,32},{48,40},{56,48},{64,56},{72,6... | collective-permute-start | bytes 393224 | tf_op jit(solution)/shard_map/while/body/eval_jaxpr/ppermute | solution.py:16
  485.9 9.0 %collective-permute-start.1 = (bf16[4,128,128]{2,1,0:T(8,128)(2,1)S(1)}, bf16[4,128,128]{2,1,0:T(8,128)(2,1)S(1)}, u32[]{:S(2)}, u32[]{:S(2)}) collective-permute-start(bf16[4,128,128]{2,1,0:T(8,128)(2,1)S(1)} %fusion.71), channel_id=1, source_target_pairs={{8,0},{16,8},{24,16},{32,24},{40,32},{48,40},{56,48},{64,56},{72,6... | collective-permute-start | bytes 393224 | tf_op jit(solution)/shard_map/while/body/eval_jaxpr/ppermute | solution.py:16
  495.0 9.0 %collective-permute-start.1 = (bf16[4,128,128]{2,1,0:T(8,128)(2,1)S(1)}, bf16[4,128,128]{2,1,0:T(8,128)(2,1)S(1)}, u32[]{:S(2)}, u32[]{:S(2)}) collective-permute-start(bf16[4,128,128]{2,1,0:T(8,128)(2,1)S(1)} %fusion.71), channel_id=1, source_target_pairs={{8,0},{16,8},{24,16},{32,24},{40,32},{48,40},{56,48},{64,56},{72,6... | collective-permute-start | bytes 393224 | tf_op jit(solution)/shard_map/while/body/eval_jaxpr/ppermute | solution.py:16
  504.1 9.3 %collective-permute-start.1 = (bf16[4,128,128]{2,1,0:T(8,128)(2,1)S(1)}, bf16[4,128,128]{2,1,0:T(8,128)(2,1)S(1)}, u32[]{:S(2)}, u32[]{:S(2)}) collective-permute-start(bf16[4,128,128]{2,1,0:T(8,128)(2,1)S(1)} %fusion.71), channel_id=1, source_target_pairs={{8,0},{16,8},{24,16},{32,24},{40,32},{48,40},{56,48},{64,56},{72,6... | collective-permute-start | bytes 393224 | tf_op jit(solution)/shard_map/while/body/eval_jaxpr/ppermute | solution.py:16
  513.6 10.5 %collective-permute-start.1 = (bf16[4,128,128]{2,1,0:T(8,128)(2,1)S(1)}, bf16[4,128,128]{2,1,0:T(8,128)(2,1)S(1)}, u32[]{:S(2)}, u32[]{:S(2)}) collective-permute-start(bf16[4,128,128]{2,1,0:T(8,128)(2,1)S(1)} %fusion.71), channel_id=1, source_target_pairs={{8,0},{16,8},{24,16},{32,24},{40,32},{48,40},{56,48},{64,56},{72,6... | collective-permute-start | bytes 393224 | tf_op jit(solution)/shard_map/while/body/eval_jaxpr/ppermute | solution.py:16
  524.3 9.0 %collective-permute-start.1 = (bf16[4,128,128]{2,1,0:T(8,128)(2,1)S(1)}, bf16[4,128,128]{2,1,0:T(8,128)(2,1)S(1)}, u32[]{:S(2)}, u32[]{:S(2)}) collective-permute-start(bf16[4,128,128]{2,1,0:T(8,128)(2,1)S(1)} %fusion.71), channel_id=1, source_target_pairs={{8,0},{16,8},{24,16},{32,24},{40,32},{48,40},{56,48},{64,56},{72,6... | collective-permute-start | bytes 393224 | tf_op jit(solution)/shard_map/while/body/eval_jaxpr/ppermute | solution.py:16
  533.4 9.0 %collective-permute-start.1 = (bf16[4,128,128]{2,1,0:T(8,128)(2,1)S(1)}, bf16[4,128,128]{2,1,0:T(8,128)(2,1)S(1)}, u32[]{:S(2)}, u32[]{:S(2)}) collective-permute-start(bf16[4,128,128]{2,1,0:T(8,128)(2,1)S(1)} %fusion.71), channel_id=1, source_target_pairs={{8,0},{16,8},{24,16},{32,24},{40,32},{48,40},{56,48},{64,56},{72,6... | collective-permute-start | bytes 393224 | tf_op jit(solution)/shard_map/while/body/eval_jaxpr/ppermute | solution.py:16
  578.2 3.9 copy-start.12
  663.9 24.0 %all-to-all-start.5 = ((bf16[16,128,4,128]{3,1,2,0:T(8,128)(2,1)}), bf16[16,128,4,128]{3,1,2,0:T(8,128)(2,1)}, u32[]{:S(2)}, u32[]{:S(2)}) async-start(bf16[16,128,4,128]{3,1,2,0:T(8,128)(2,1)} %get-tuple-element.174), calls=%async_computation.5 | async-start | bytes 4194304 | tf_op jit(solution)/shard_map/all_to_all | solution.py:250
where the time goes:
time: 712 us; the launch traced here: 705 us
  waiting for transfers between devices  243 us (34%)
  blocking collectives  136 us (19%)
  starting transfers between devices  128 us (18%)
  local copies, waits for them, and re-layouts  119 us (17%)
  matrix products  41.3 us (6%)
  other arithmetic  35 us (5%)
    ppermute x30, waiting for transfers between devices, from_behind(): return lax.ppermute(block, axis, route)  161 us
    ppermute x30, starting transfers between devices, from_behind(): return lax.ppermute(block, axis, route)  102 us
    all_to_all x1, blocking collectives, shards(): lax.all_to_all(homeward(value_grad), 'seq', split_axis=0, concat_axis=0,...  42.8 us
    all_to_all x1, blocking collectives, shards(): lax.all_to_all(outgoing(out_cotangent), 'seq', split_axis=0, concat_axis=...  35 us
    all_to_all x1, blocking collectives, shards(): lax.all_to_all(homeward(key_grad), 'seq', split_axis=0, concat_axis=0, ti...  34.9 us
    all_to_all x1, waiting for transfers between devices, shards(): lax.all_to_all(outgoing(query_rows), 'seq', split_axis=0, concat_axis=0,...  27.3 us
    all_to_all x1, waiting for transfers between devices, shards(): lax.all_to_all(outgoing(value_rows), 'seq', split_axis=0, concat_axis=0,...  26 us
    psum x1, blocking collectives, cotangent_of(): squares, crossed = lax.psum((squares, crossed), 'head')  23.8 us
  transfers between devices with their start and end apart: 35, of which 34 were waited for; matrix products, arithmetic and copies ran while one was open for 9% of the time, Pallas kernels for 0%

commit v1 on v0

v1 whole, which is shorter than its diff:
```python
import functools

import jax
import jax.numpy as jnp
from jax import lax
from jax.experimental import pallas as pl
from jax.experimental.pallas import tpu as pltpu
from jax.sharding import PartitionSpec as P

HEAD = 128
GROUP = 128
RING = 4
EPSILON = 1e-06
MESH = pl.DeviceIdType.MESH
F32 = jnp.float32
BF16 = jnp.bfloat16


def dot(a, b, dims):
    return lax.dot_general(a, b, (dims, ((), ())), preferred_element_type=F32)


NN = ((1,), (0,))
NT = ((1,), (1,))
TN = ((0,), (0,))


def head_cols(h):
    return slice(h * HEAD, (h + 1) * HEAD)


def decay_tables(rate_ref, heads, dec_ref=None, qdec_ref=None, kdec_ref=None):
    row = lax.broadcasted_iota(jnp.int32, (GROUP, GROUP), 0).astype(F32)
    col = lax.broadcasted_iota(jnp.int32, (GROUP, GROUP), 1).astype(F32)
    for h in range(heads):
        r = rate_ref[h]
        if dec_ref is not None:
            spread = row - col
            dec_ref[h] = jnp.where(spread >= 0.0, jnp.exp(-r * jnp.maximum(spread, 0.0)), 0.0)
        if qdec_ref is not None:
            qdec_ref[h] = jnp.exp(-r * (row + 1.0))
        if kdec_ref is not None:
            kdec_ref[h] = jnp.exp(-r * (GROUP - 1.0 - row))


def seg_tiles(seg_ref):
    row = jnp.broadcast_to(seg_ref[0], (GROUP, GROUP))
    return row, row.T


def summary_kernel(heads, rate_ref, edge_ref, seg_ref, k_ref, v_ref, s_ref, kdec_ref):
    i = pl.program_id(0)

    @pl.when(i == 0)
    def _():
        decay_tables(rate_ref, heads, kdec_ref=kdec_ref)

    _, seg_c = seg_tiles(seg_ref)
    live = seg_c == edge_ref[1, i]
    for h in range(heads):
        side = jnp.where(live, kdec_ref[h], 0.0)
        weighted = (side * v_ref[:, head_cols(h)].astype(F32)).astype(BF16)
        s = dot(k_ref[:, head_cols(h)], weighted, TN).astype(BF16)
        s_ref[RING * h : RING * (h + 1), 0] = s.reshape(RING, HEAD // RING, HEAD)


def output_kernel(
    heads, rate_ref, edge_ref, seg_ref, q_ref, k_ref, v_ref, u_ref, p_ref, gain_ref,
    o_ref, sums_ref, dec_ref, qdec_ref,
):
    i = pl.program_id(0)

    @pl.when(i == 0)
    def _():
        decay_tables(rate_ref, heads, dec_ref=dec_ref, qdec_ref=qdec_ref)
        sums_ref[...] = jnp.zeros_like(sums_ref)

    seg_r, seg_c = seg_tiles(seg_ref)
    same = seg_r == seg_c
    live = seg_c == edge_ref[0, i]
    squares = jnp.zeros((GROUP, HEAD), F32)
    crossed = jnp.zeros((GROUP, HEAD), F32)
    for h in range(heads):
        cols = head_cols(h)
        q = q_ref[:, cols]
        mixing = (dot(q, k_ref[:, cols], NT) * jnp.where(same, dec_ref[h], 0.0)).astype(BF16)
        prev = p_ref[RING * h : RING * (h + 1), 0].reshape(HEAD, HEAD)
        out = dot(mixing, v_ref[:, cols], NN) + jnp.where(live, qdec_ref[h], 0.0) * dot(q, prev, NN)
        o_ref[:, cols] = out
        squares += out * out
        crossed += gain_ref[:, cols] * u_ref[:, cols].astype(F32) * out
    lane = lax.broadcasted_iota(jnp.int32, (GROUP, HEAD), 1)
    squares = jnp.sum(squares, axis=1, keepdims=True)
    crossed = jnp.sum(crossed, axis=1, keepdims=True)
    groups = pl.num_programs(0)
    sums_ref[...] += jnp.where(lane == i, squares, 0.0) + jnp.where(lane == i + groups, crossed, 0.0)


def cotangent_kernel(
    heads, channels, rate_ref, edge_ref, seg_ref, q_ref, u_ref, o_ref, gain_ref, sums_ref,
    g_ref, r_ref, qdec_ref,
):
    i = pl.program_id(0)

    @pl.when(i == 0)
    def _():
        decay_tables(rate_ref, heads, qdec_ref=qdec_ref)

    _, seg_c = seg_tiles(seg_ref)
    live = seg_c == edge_ref[0, i]
    lane = lax.broadcasted_iota(jnp.int32, (GROUP, HEAD), 1)
    groups = pl.num_programs(0)
    sums = sums_ref[...]
    squares = jnp.sum(jnp.where(lane == i, sums, 0.0), axis=1, keepdims=True)
    crossed = jnp.sum(jnp.where(lane == i + groups, sums, 0.0), axis=1, keepdims=True)
    scaling = lax.rsqrt(squares / channels + EPSILON)
    back = scaling * scaling * scaling * (crossed / channels)
    for h in range(heads):
        cols = head_cols(h)
        g = (scaling * (gain_ref[:, cols] * u_ref[:, cols].astype(F32)) - back * o_ref[:, cols]).astype(BF16)
        g_ref[:, cols] = g
        weighted = (jnp.where(live, qdec_ref[h], 0.0) * g.astype(F32)).astype(BF16)
        r = dot(q_ref[:, cols], weighted, TN).astype(BF16)
        r_ref[RING * h : RING * (h + 1), 0] = r.reshape(RING, HEAD // RING, HEAD)


def gradient_kernel(
    heads, rate_ref, edge_ref, seg_ref, q_ref, k_ref, v_ref, g_ref, p_ref, a_ref,
    qg_ref, kg_ref, vg_ref, dec_ref, qdec_ref, kdec_ref,
):
    i = pl.program_id(0)

    @pl.when(i == 0)
    def _():
        decay_tables(rate_ref, heads, dec_ref, qdec_ref, kdec_ref)

    seg_r, seg_c = seg_tiles(seg_ref)
    same = seg_r == seg_c
    live_q = seg_c == edge_ref[0, i]
    live_k = seg_c == edge_ref[1, i]
    for h in range(heads):
        cols = head_cols(h)
        q, k, v, g = q_ref[:, cols], k_ref[:, cols], v_ref[:, cols], g_ref[:, cols]
        prev = p_ref[RING * h : RING * (h + 1), 0].reshape(HEAD, HEAD)
        after = a_ref[RING * h : RING * (h + 1), 0].reshape(HEAD, HEAD)
        mask = jnp.where(same, dec_ref[h], 0.0)
        mixing = (dot(q, k, NT) * mask).astype(BF16)
        score = (dot(g, v, NT) * mask).astype(BF16)
        side_q = jnp.where(live_q, qdec_ref[h], 0.0)
        side_k = jnp.where(live_k, kdec_ref[h], 0.0)
        qg_ref[:, cols] = (dot(score, k, NN) + side_q * dot(g, prev, NT)).astype(BF16)
        kg_ref[:, cols] = (dot(score, q, TN) + side_k * dot(v, after, NT)).astype(BF16)
        vg_ref[:, cols] = (dot(mixing, g, TN) + side_k * dot(k, after, NN)).astype(BF16)


def torus_offsets(ring):
    offsets = [(dy, dz) for dy in range(ring) for dz in range(ring) if (dy, dz) != (0, 0)]
    return sorted(offsets, key=lambda o: min(o[0], ring - o[0]) + min(o[1], ring - o[1]))


def scan_kernel(
    ring, reverse, order_ref, home_ref, carry_ref, s_ref, p_ref,
    got_ref, seq_ref, back_ref, send1, recv1, send2, recv2, local_sem,
):
    me = lax.axis_index("seq")
    head = lax.axis_index("head")
    y, z = me // ring, lax.rem(me, ring)
    peers = [lax.rem(y + dy, ring) * ring + lax.rem(z + dz, ring) for dy, dz in torus_offsets(ring)]
    count = len(peers)
    per = got_ref.shape[0] // (count + 1)
    barrier = pltpu.get_barrier_semaphore()
    for peer in peers:
        pl.semaphore_signal(barrier, inc=1, device_id=(peer, head), device_id_type=MESH)
    own = pltpu.make_async_copy(s_ref.at[me], got_ref.at[pl.ds(me * per, per)], local_sem.at[0])
    own.start()
    pl.semaphore_wait(barrier, count)
    copies = []
    for n, peer in enumerate(peers):
        copy = pltpu.make_async_remote_copy(
            src_ref=s_ref.at[peer], dst_ref=got_ref.at[pl.ds(me * per, per)],
            send_sem=send1.at[n], recv_sem=recv1.at[n],
            device_id=(peer, head), device_id_type=MESH,
        )
        copy.start()
        copies.append(copy)
    own.wait()
    for copy in copies:
        copy.wait()
    groups = got_ref.shape[0]
    unroll = 8

    def step(b, state):
        for n in range(unroll):
            t = b * unroll + n
            if reverse:
                t = groups - 1 - t
            seq_ref[t] = state.astype(BF16)
            state = carry_ref[t] * state + got_ref[order_ref[t]].astype(F32)
        return state

    lax.fori_loop(0, groups // unroll, step, jnp.zeros(got_ref.shape[1:], F32))

    def put(b, _):
        for n in range(unroll):
            p = b * unroll + n
            back_ref[p] = seq_ref[home_ref[p]]
        return 0

    lax.fori_loop(0, groups // unroll, put, 0)
    own = pltpu.make_async_copy(back_ref.at[pl.ds(me * per, per)], p_ref.at[me], local_sem.at[1])
    own.start()
    copies = []
    for n, peer in enumerate(peers):
        copy = pltpu.make_async_remote_copy(
            src_ref=back_ref.at[pl.ds(peer * per, per)], dst_ref=p_ref.at[me],
            send_sem=send2.at[n], recv_sem=recv2.at[n],
            device_id=(peer, head), device_id_type=MESH,
        )
        copy.start()
        copies.append(copy)
    own.wait()
    for copy in copies:
        copy.wait()


def total_kernel(x_ref, o_ref, mine_ref, got_ref, send, recv):
    size = lax.axis_size("head")
    me = lax.axis_index("head")
    seq = lax.axis_index("seq")
    peers = [lax.rem(me + n, size) for n in range(1, size)]
    barrier = pltpu.get_barrier_semaphore()
    for peer in peers:
        pl.semaphore_signal(barrier, inc=1, device_id=(seq, peer), device_id_type=MESH)
    part = mine_ref.shape[0]
    packed = x_ref[0:part]
    for n in range(1, GROUP // part):
        packed = packed + pltpu.roll(x_ref[part * n : part * (n + 1)], n * part, 1)
    mine_ref[...] = packed
    pl.semaphore_wait(barrier, size - 1)
    copies = []
    for n, peer in enumerate(peers):
        copy = pltpu.make_async_remote_copy(
            src_ref=mine_ref, dst_ref=got_ref.at[n], send_sem=send.at[n], recv_sem=recv.at[n],
            device_id=(seq, peer), device_id_type=MESH,
        )
        copy.start()
        copies.append(copy)
    for copy in copies:
        copy.wait()
    total = mine_ref[...]
    for n in range(size - 1):
        total = total + got_ref[n]
    o_ref[0:part] = total
    for n in range(1, GROUP // part):
        o_ref[part * n : part * (n + 1)] = pltpu.roll(total, HEAD - n * part, 1)


def shards(q, k, v, u, gain, rate, lengths, home):
    devices = lax.axis_size("seq")
    sides = lax.axis_size("head")
    me = lax.axis_index("seq")
    heads = q.shape[1] // HEAD
    groups = home.shape[0]
    rows, width = q.shape
    docs = lengths.shape[0]
    ids = jnp.arange(docs, dtype=jnp.int32)
    ends = jnp.sum(jnp.where(ids[None, :] <= ids[:, None], lengths[None, :], 0), axis=1)

    def segment(pos):
        return jnp.sum((ends <= pos[..., None]).astype(jnp.int32), axis=-1)

    seg = segment(home[:, None] * GROUP + jnp.arange(GROUP, dtype=jnp.int32)[None, :]).astype(F32)
    before = jnp.where(home == 0, -1, segment(home * GROUP - 1)).astype(F32)
    last = segment(home * GROUP + GROUP - 1).astype(F32)
    edges = jnp.stack([before, last])
    seg = seg.reshape(groups, 1, GROUP)

    homes = lax.all_gather(home, "seq", tiled=True)
    total_groups = devices * groups
    steps = jnp.arange(total_groups, dtype=jnp.int32)
    order = jnp.sum(jnp.where(homes[None, :] == steps[:, None], steps[None, :], 0), axis=1)
    owner_head = me // RING
    own_rate = jnp.sum(jnp.where(jnp.arange(heads) == owner_head, rate, 0.0))
    joined = (steps == 0) | (segment(steps * GROUP - 1) == segment(steps * GROUP + GROUP - 1))
    carry = jnp.where(joined, jnp.exp(-own_rate * GROUP), 0.0)

    smem = pl.BlockSpec(memory_space=pltpu.SMEM)
    seg_spec = pl.BlockSpec((1, 1, GROUP), lambda i: (i, 0, 0))
    row_spec = pl.BlockSpec((GROUP, width), lambda i: (i, 0))
    state_spec = pl.BlockSpec((devices, 1, HEAD // RING, HEAD), lambda i: (0, i, 0, 0))
    gain_spec = pl.BlockSpec((1, width), lambda i: (0, 0))
    sums_spec = pl.BlockSpec((GROUP, HEAD), lambda i: (0, 0))
    table = pltpu.VMEM((heads, GROUP, GROUP), F32)
    state_shape = jax.ShapeDtypeStruct((devices, groups, HEAD // RING, HEAD), BF16)
    rows_shape = jax.ShapeDtypeStruct((rows, width), BF16)
    gain = gain.reshape(1, width)
    params = pltpu.CompilerParams(vmem_limit_bytes=40 << 20)

    def exchange(states, reverse, ident):
        dma = pltpu.SemaphoreType.DMA
        return pl.pallas_call(
            functools.partial(scan_kernel, RING, reverse),
            out_shape=state_shape,
            in_specs=[smem, smem, smem, pl.BlockSpec(memory_space=pl.ANY)],
            out_specs=pl.BlockSpec(memory_space=pl.ANY),
            scratch_shapes=[pltpu.VMEM((total_groups, HEAD // RING, HEAD), BF16)] * 3
            + [dma((devices - 1,))] * 4
            + [dma((2,))],
            compiler_params=pltpu.CompilerParams(
                collective_id=ident, has_side_effects=True, vmem_limit_bytes=40 << 20
            ),
        )(order, homes, carry, states)

    summaries = pl.pallas_call(
        functools.partial(summary_kernel, heads),
        grid=(groups,),
        out_shape=state_shape,
        in_specs=[smem, smem, seg_spec, row_spec, row_spec],
        out_specs=state_spec,
        scratch_shapes=[table],
        compiler_params=params,
    )(rate, edges, seg, k, v)
    prev = exchange(summaries, False, 0)
    out, sums = pl.pallas_call(
        functools.partial(output_kernel, heads),
        grid=(groups,),
        out_shape=(jax.ShapeDtypeStruct((rows, width), F32), jax.ShapeDtypeStruct((GROUP, HEAD), F32)),
        in_specs=[smem, smem, seg_spec, row_spec, row_spec, row_spec, row_spec, state_spec, gain_spec],
        out_specs=(row_spec, sums_spec),
        scratch_shapes=[table, table],
        compiler_params=params,
    )(rate, edges, seg, q, k, v, u, prev, gain)
    part = 2 * groups
    whole = pl.BlockSpec(memory_space=pltpu.VMEM)
    sums = pl.pallas_call(
        total_kernel,
        out_shape=jax.ShapeDtypeStruct((GROUP, HEAD), F32),
        in_specs=[whole],
        out_specs=whole,
        scratch_shapes=[
            pltpu.VMEM((part, HEAD), F32),
            pltpu.VMEM((sides - 1, part, HEAD), F32),
            pltpu.SemaphoreType.DMA((sides - 1,)),
            pltpu.SemaphoreType.DMA((sides - 1,)),
        ],
        compiler_params=pltpu.CompilerParams(collective_id=2, has_side_effects=True),
    )(sums)
    grad, rev = pl.pallas_call(
        functools.partial(cotangent_kernel, heads, width * sides),
        grid=(groups,),
        out_shape=(rows_shape, state_shape),
        in_specs=[smem, smem, seg_spec, row_spec, row_spec, row_spec, gain_spec, sums_spec],
        out_specs=(row_spec, state_spec),
        scratch_shapes=[table],
        compiler_params=params,
    )(rate, edges, seg, q, u, out, gain, sums)
    after = exchange(rev, True, 1)
    return pl.pallas_call(
        functools.partial(gradient_kernel, heads),
        grid=(groups,),
        out_shape=(rows_shape,) * 3,
        in_specs=[smem, smem, seg_spec, row_spec, row_spec, row_spec, row_spec, state_spec, state_spec],
        out_specs=(row_spec,) * 3,
        scratch_shapes=[table] * 3,
        compiler_params=params,
    )(rate, edges, seg, q, k, v, grad, prev, after)


def solution(mesh):
    rows = P("seq", "head")
    return jax.shard_map(
        shards,
        mesh=mesh,
        in_specs=(rows, rows, rows, rows, P("head"), P("head"), P(), P("seq")),
        out_specs=(rows, rows, rows),
        check_vma=False,
    )
```

time: 712 us -> 201 us (0.28)
  waiting for transfers between devices: 243 us -> 0 us
  Pallas kernels: 0 us -> 166 us
  starting transfers between devices: 128 us -> 0 us
  blocking collectives: 136 us -> 17.5 us
  local copies, waits for them, and re-layouts: 119 us -> 11.2 us
  matrix products: 41.3 us -> 0 us
  other arithmetic: 35 us -> 3.95 us
    pallas_call x0 -> x7, Pallas kernels: none -> 166 us  [the longest x2 116 us: exchange(): pl.pallas_call(functools.partial(scan_kernel, RING, reverse), out_shape=s...]
    ppermute x30 -> x0, waiting for transfers between devices: 161 us -> none  [from_behind(): return lax.ppermute(block, axis, route)]
    all_to_all x3 -> x0, blocking collectives: 113 us -> none  [the longest x1 42.8 us: shards(): lax.all_to_all(homeward(value_grad), 'seq', split_axis=0, concat_axis=0,...]
    ppermute x30 -> x0, starting transfers between devices: 102 us -> none  [from_behind(): return lax.ppermute(block, axis, route)]
    all_to_all x5 -> x0, waiting for transfers between devices: 81.4 us -> none  [the longest x1 27.3 us: shards(): lax.all_to_all(outgoing(query_rows), 'seq', split_axis=0, concat_axis=0,...]
    gather x15 -> x0, local copies, waits for them, and re-layouts: 49 us -> none  [the longest x4 13.7 us: outgoing(): return jnp.take(rows.reshape(group_shape), picked, axis=0)]
    dot_general x12 -> x0, matrix products: 41.3 us -> none  [the longest x1 7.6 us: output_local(): jnp.einsum('cjhd,chde->cjhe', query_c, prev_states, preferred_element_typ...]
    reshape x9 -> x0, local copies, waits for them, and re-layouts: 26.6 us -> none  [the longest x8 23.7 us: outgoing(): return jnp.take(rows.reshape(group_shape), picked, axis=0)]
  transfers between devices with their start and end apart: 35 -> 0, of which waited for: 34 -> 0; matrix products, arithmetic and copies ran while one was open for 9% -> 0% of each run, Pallas kernels for 0% -> 0%
where the time goes in v1:
time: 201 us
  Pallas kernels  166 us (83%)
  blocking collectives  17.5 us (9%)
  local copies, waits for them, and re-layouts  11.2 us (6%)
  other arithmetic  3.95 us (2%)
  between operations  2.21 us (1%)
    pallas_call x2, Pallas kernels, exchange(): pl.pallas_call(functools.partial(scan_kernel, RING, reverse), out_shape=s...  116 us
    pallas_call x1, Pallas kernels, shards(): pl.pallas_call(functools.partial(gradient_kernel, heads), grid=(groups,),...  19.6 us
    unnamed x1, blocking collectives  17.5 us
    unnamed x35, local copies, waits for them, and re-layouts  11.2 us
    pallas_call x1, Pallas kernels, shards(): pl.pallas_call(functools.partial(output_kernel, heads), grid=(groups,), o...  10.3 us
    pallas_call x1, Pallas kernels, shards(): pl.pallas_call(total_kernel, out_shape=jax.ShapeDtypeStruct((GROUP, HEAD)...  8.14 us
    pallas_call x1, Pallas kernels, shards(): pl.pallas_call(functools.partial(cotangent_kernel, heads, width * sides),...  6.47 us
    pallas_call x1, Pallas kernels, shards(): pl.pallas_call(functools.partial(summary_kernel, heads), grid=(groups,),...  5.31 us

profile of v1, /device:TPU:0, one launch (start us, length us, event | category | flops | bytes accessed | tf_op | source)
XLA Modules:
  0.0 200.6 jit_solution(13367663666190654089)
XLA Ops:
  0.6 1.3 fusion.4
  2.6 1.2 dynamic-slice
  4.5 0.8 select_reduce_fusion.1
  5.3 0.9 dynamic-update-slice
  6.1 17.5 %all-reduce.home_ref = s32[256]{0:T(256)S(1)} all-reduce(s32[256]{0:T(256)S(1)} %dynamic-update-slice), channel_id=1, replica_groups=mesh['seq'=16,'head'=8] {'seq'}, use_global_device_ids=true, to_apply=%add | all-reduce | flops 256 | bytes 2048
  23.6 0.1 select_reduce_fusion.order_ref
  23.7 0.7 broadcast_multiply_fusion
  24.4 0.2 convert_reduce_fusion.4
  24.6 0.7 fusion.3
  25.3 0.1 convert_reduce_fusion.1
  25.4 0.1 iota_add_fusion
  25.4 0.1 convert_reduce_fusion
  25.6 0.0 copy-start.3
  25.6 1.6 copy-done.3
  27.1 0.0 copy-start.6
  27.2 1.6 copy-done.6
  28.7 0.0 copy-start.13
  28.7 0.7 copy-done.13
  29.4 0.0 copy-start.8
  29.4 5.3 %shard_map.103.s_ref = bf16[16,16,32,128]{3,2,1,0:T(8,128)(2,1)S(1)} custom-call(f32[4]{0:T(128)S(1)} %copy-done.13, f32[2,16]{1,0:T(2,128)S(1)} %pad_maximum_fusion.edge_ref, f32[16,1,128]{2,1,0:T(1,128)S(1)} %bitcast.7, bf16[2048,512]{1,0:T(8,128)(2,1)S(1)} %copy-done.3, bf16[2048,512]{1,0:T(8,128)(2,1)S(1)} %copy-done.6), custom_call_target="tpu_custom_call" | custom-call | tf_op jit(solution)/shard_map/pallas_call | solution.py:314
  34.7 0.0 copy-start
  34.7 0.0 copy-start.4
  34.7 0.0 copy-start.15
  34.7 53.2 %shard_map.104.p_ref = bf16[16,16,32,128]{3,2,1,0:T(8,128)(2,1)S(1)} custom-call(s32[256]{0:T(256)S(1)} %select_reduce_fusion.order_ref, s32[256]{0:T(256)S(1)} %all-reduce.home_ref, f32[256]{0:T(256)S(1)} %or_select_fusion.carry_ref, bf16[16,16,32,128]{3,2,1,0:T(8,128)(2,1)S(1)} %shard_map.103.s_ref), custom_call_target="tpu_custom_call" | custom-call | tf_op jit(solution)/shard_map/pallas_call | solution.py:301
  87.9 0.0 copy-done.8
  87.9 0.0 copy-done
  88.0 0.0 copy-done.4
  88.0 0.0 copy-done.15
  88.0 0.0 copy-start.1
  88.0 0.0 copy-start.14
  88.0 10.3 %shard_map.105 = (f32[2048,512]{1,0:T(8,128)}, f32[128,128]{1,0:T(8,128)S(1)}) custom-call(f32[4]{0:T(128)S(1)} %copy-done.13, f32[2,16]{1,0:T(2,128)S(1)} %pad_maximum_fusion.edge_ref, f32[16,1,128]{2,1,0:T(1,128)S(1)} %bitcast.8, bf16[2048,512]{1,0:T(8,128)(2,1)S(1)} %copy-done, bf16[2048,512]{1,0:T(8,128)(2,1)S(1)} %copy-done.4, ...), custom_call_target="tpu_custom_call" | custom-call | tf_op jit(solution)/shard_map/pallas_call | solution.py:324
  98.3 0.0 copy-done.1
  98.3 0.0 copy-start.12
  98.3 0.6 copy-done.12
  98.9 8.1 %shard_map.106.sums_ref = f32[128,128]{1,0:T(8,128)} custom-call(f32[128,128]{1,0:T(8,128)} %copy-done.12), custom_call_target="tpu_custom_call" | custom-call | tf_op jit(solution)/shard_map/pallas_call | solution.py:335
  107.0 0.0 copy-done.14
  107.1 0.0 copy-start.9
  107.1 1.6 copy-done.9
  108.7 0.0 copy-start.10
  108.7 2.2 %copy-done.10 = f32[2048,512]{1,0:T(8,128)S(1)} copy-done((f32[2048,512]{1,0:T(8,128)S(1)}, f32[2048,512]{1,0:T(8,128)}, u32[]{:S(2)}) %copy-start.10) | copy-done | bytes 4194328
  110.8 0.0 copy-start.11
  110.8 0.8 copy-done.11
  111.7 0.0 copy-start.7
  111.7 6.5 %shard_map.107 = (bf16[2048,512]{1,0:T(8,128)(2,1)S(1)}, bf16[16,16,32,128]{3,2,1,0:T(8,128)(2,1)S(1)}) custom-call(f32[4]{0:T(128)S(1)} %copy-done.14, f32[2,16]{1,0:T(2,128)S(1)} %pad_maximum_fusion.edge_ref, f32[16,1,128]{2,1,0:T(1,128)S(1)} %bitcast.9, bf16[2048,512]{1,0:T(8,128)(2,1)S(1)} %copy-done, bf16[2048,512]{1,0:T(8,128)(2,1)S(1)} %copy-done.9, ...), custom_call_target="tpu_custom_call" | custom-call | tf_op jit(solution)/shard_map/pallas_call | solution.py:348
  118.2 0.0 copy-start.2
  118.2 0.0 copy-start.5
  118.2 62.8 %shard_map.108.a_ref = bf16[16,16,32,128]{3,2,1,0:T(8,128)(2,1)S(1)} custom-call(s32[256]{0:T(256)S(1)} %select_reduce_fusion.order_ref, s32[256]{0:T(256)S(1)} %all-reduce.home_ref, f32[256]{0:T(256)S(1)} %or_select_fusion.carry_ref, bf16[16,16,32,128]{3,2,1,0:T(8,128)(2,1)S(1)} %get-tuple-element.10.s_ref), custom_call_target="tpu_custom_call" | custom-call | tf_op jit(solution)/shard_map/pallas_call | solution.py:301
  181.0 0.0 copy-done.7
  181.0 0.0 copy-done.2
  181.0 0.0 copy-done.5
  181.0 19.6 %shard_map.109 = (bf16[2048,512]{1,0:T(8,128)(2,1)}, bf16[2048,512]{1,0:T(8,128)(2,1)}, bf16[2048,512]{1,0:T(8,128)(2,1)}) custom-call(f32[4]{0:T(128)S(1)} %copy-done.14, f32[2,16]{1,0:T(2,128)S(1)} %pad_maximum_fusion.edge_ref, f32[16,1,128]{2,1,0:T(1,128)S(1)} %bitcast.10, bf16[2048,512]{1,0:T(8,128)(2,1)S(1)} %copy-done, ...), custom_call_target="tpu_custom_call" | custom-call | tf_op jit(solution)/shard_map/pallas_call | solution.py:358
  (5 shorter events, 0.0 us)
Async XLA Ops:
  25.6 1.6 copy-start.3
  27.1 1.6 copy-start.6
  28.7 0.7 copy-start.13
  29.4 58.5 %copy-start.8 = (bf16[2048,512]{1,0:T(8,128)(2,1)S(1)}, bf16[2048,512]{1,0:T(8,128)(2,1)}, u32[]{:S(2)}) copy-start(bf16[2048,512]{1,0:T(8,128)(2,1)} %u_ref.3) | copy-start | bytes 6291460
  34.7 53.2 %copy-start = (bf16[2048,512]{1,0:T(8,128)(2,1)S(1)}, bf16[2048,512]{1,0:T(8,128)(2,1)}, u32[]{:S(2)}) copy-start(bf16[2048,512]{1,0:T(8,128)(2,1)} %q_ref.5) | copy-start | bytes 6291460
  34.7 53.2 %copy-start.4 = (bf16[2048,512]{1,0:T(8,128)(2,1)S(1)}, bf16[2048,512]{1,0:T(8,128)(2,1)}, u32[]{:S(2)}) copy-start(bf16[2048,512]{1,0:T(8,128)(2,1)} %k_ref.5) | copy-start | bytes 6291460
  34.7 53.2 %copy-start.15 = (f32[512]{0:T(512)S(1)}, f32[512]{0:T(512)}, u32[]{:S(2)}) copy-start(f32[512]{0:T(512)} %param.12) | copy-start | bytes 6148
  88.0 10.3 %copy-start.1 = (bf16[16,16,32,128]{3,2,1,0:T(8,128)(2,1)}, bf16[16,16,32,128]{3,2,1,0:T(8,128)(2,1)S(1)}, u32[]{:S(2)}) copy-start(bf16[16,16,32,128]{3,2,1,0:T(8,128)(2,1)S(1)} %shard_map.104.p_ref) | copy-start | bytes 6291460
  88.0 19.1 %copy-start.14 = (f32[4]{0:T(128)S(1)}, f32[4]{0:T(128)}, u32[]{:S(2)}) copy-start(f32[4]{0:T(128)} %rate_ref.7) | copy-start | bytes 52
  98.3 0.6 copy-start.12
  107.1 1.6 copy-start.9
  108.7 2.2 %copy-start.10 = (f32[2048,512]{1,0:T(8,128)S(1)}, f32[2048,512]{1,0:T(8,128)}, u32[]{:S(2)}) copy-start(f32[2048,512]{1,0:T(8,128)} %get-tuple-element.7.o_ref) | copy-start | bytes 12582916
  110.8 0.8 copy-start.11
  111.7 69.3 %copy-start.7 = (bf16[2048,512]{1,0:T(8,128)(2,1)S(1)}, bf16[2048,512]{1,0:T(8,128)(2,1)}, u32[]{:S(2)}) copy-start(bf16[2048,512]{1,0:T(8,128)(2,1)} %v_ref.5) | copy-start | bytes 6291460
  118.2 62.9 %copy-start.2 = (bf16[16,16,32,128]{3,2,1,0:T(8,128)(2,1)S(1)}, bf16[16,16,32,128]{3,2,1,0:T(8,128)(2,1)}, u32[]{:S(2)}) copy-start(bf16[16,16,32,128]{3,2,1,0:T(8,128)(2,1)} %copy-done.1) | copy-start | bytes 6291460
  118.2 62.9 %copy-start.5 = (bf16[2048,512]{1,0:T(8,128)(2,1)S(1)}, bf16[2048,512]{1,0:T(8,128)(2,1)}, u32[]{:S(2)}) copy-start(bf16[2048,512]{1,0:T(8,128)(2,1)} %k_ref.5) | copy-start | bytes 6291460

commit v2 on v0

v2 whole, which is shorter than its diff:
```python
import functools

import jax
import jax.numpy as jnp
from jax import lax
from jax.experimental import pallas as pl
from jax.experimental.pallas import tpu as pltpu
from jax.sharding import PartitionSpec as P

HEAD = 128
GROUP = 128
RING = 4
CHUNK = 4
UNROLL = 8
EPSILON = 1e-06
MESH = pl.DeviceIdType.MESH
F32 = jnp.float32
BF16 = jnp.bfloat16
I32 = jnp.int32
NN = ((1,), (0,))
NT = ((1,), (1,))
TN = ((0,), (0,))


def dot(a, b, dims):
    return lax.dot_general(a, b, (dims, ((), ())), preferred_element_type=F32)


def cols_of(h):
    return slice(h * HEAD, (h + 1) * HEAD)


def iota(shape, dim):
    return lax.broadcasted_iota(I32, shape, dim)


def torus_offsets(ring):
    offsets = [(dy, dz) for dy in range(ring) for dz in range(ring) if (dy, dz) != (0, 0)]
    return sorted(offsets, key=lambda o: min(o[0], ring - o[0]) + min(o[1], ring - o[1]))


def wait_bytes(ref, sem):
    pltpu.make_async_copy(ref, ref, sem).wait()


def fused_kernel(
    heads, groups, devices, sides, docs,
    rate_ref, len_ref, home_ref, gain_ref, q_hbm, k_hbm, v_hbm, u_hbm,
    qo_hbm, ko_hbm, vo_hbm,
    q_ref, k_ref, v_ref, u_ref, send_ref, got1_ref, got2_ref, seq_ref, back_ref, prev_ref, after_ref,
    att_ref, vgp_ref, mix_ref, qout_ref, kout_ref, vout_ref,
    dec_ref, qdec_ref, kdec_ref, segr_ref, bef_ref, last_ref, segc_ref,
    hmine_ref, hall_ref, hcomp_ref, order_ref, carry_ref, homes_s, order_s, carry_s,
    mine_ref, gsum_ref,
    kv_sem, qu_sem, own_sem, smem_sem, hsend, hrecv, send1, recv1, send2, recv2,
    send3, recv3, send4, recv4, ssend, srecv, out_sem,
):
    me = lax.axis_index("seq")
    side = lax.axis_index("head")
    y, z = me // RING, lax.rem(me, RING)
    peers = [lax.rem(y + dy, RING) * RING + lax.rem(z + dz, RING) for dy, dz in torus_offsets(RING)]
    mates = [lax.rem(side + n, sides) for n in range(1, sides)]
    others = devices - 1
    total = devices * groups
    chunks = groups // CHUNK
    slab = CHUNK * GROUP
    part = HEAD // RING

    barrier = pltpu.get_barrier_semaphore()
    for peer in peers:
        pl.semaphore_signal(barrier, inc=1, device_id=(peer, side), device_id_type=MESH)
    for mate in mates:
        pl.semaphore_signal(barrier, inc=1, device_id=(me, mate), device_id_type=MESH)

    def slab_copy(hbm, ref, c, sem):
        rows = pl.ds(c * slab, slab)
        return pltpu.make_async_copy(hbm.at[rows], ref.at[rows], sem)

    for c in range(chunks):
        slab_copy(k_hbm, k_ref, c, kv_sem.at[0, c]).start()
        slab_copy(v_hbm, v_ref, c, kv_sem.at[1, c]).start()
    load_q = pltpu.make_async_copy(q_hbm, q_ref, qu_sem.at[0])
    load_u = pltpu.make_async_copy(u_hbm, u_ref, qu_sem.at[1])
    load_q.start()
    load_u.start()

    row = iota((GROUP, GROUP), 0).astype(F32)
    spread = row - iota((GROUP, GROUP), 1).astype(F32)
    for h in range(heads):
        r = rate_ref[h]
        dec_ref[h] = jnp.where(spread >= 0.0, jnp.exp(-r * jnp.maximum(spread, 0.0)), 0.0)
        qdec_ref[h] = jnp.exp(-r * (row + 1.0))
        kdec_ref[h] = jnp.exp(-r * (GROUP - 1.0 - row))

    home_rows = jnp.zeros((groups, HEAD), I32)
    home_lanes = jnp.zeros((8, HEAD), I32)
    group_row = iota((groups, HEAD), 0)
    lane8 = iota((8, HEAD), 1)
    for i in range(groups):
        home_rows = jnp.where(group_row == i, home_ref[i], home_rows)
        home_lanes = jnp.where(lane8 == i, home_ref[i], home_lanes)
    hmine_ref[...] = home_lanes
    hall_ref[me] = home_lanes
    steps = iota((8, HEAD), 0) * HEAD + lane8
    pos = home_rows * GROUP + iota((groups, HEAD), 1)
    pos_b = home_rows * GROUP - 1
    step_b = steps * GROUP - 1
    seg = jnp.zeros_like(pos)
    seg_b = jnp.zeros_like(pos)
    step_seg_b = jnp.zeros_like(steps)
    step_seg_e = jnp.zeros_like(steps)
    end = jnp.int32(0)
    for n in range(docs):
        end = end + len_ref[n]
        seg += (pos >= end).astype(I32)
        seg_b += (pos_b >= end).astype(I32)
        step_seg_b += (step_b >= end).astype(I32)
        step_seg_e += (step_b + GROUP >= end).astype(I32)
    seg_b = jnp.where(home_rows == 0, -1, seg_b).astype(F32)
    seg = seg.astype(F32)
    for i in range(groups):
        segr_ref[i] = seg[i : i + 1]
        bef_ref[i] = seg_b[i : i + 1]
        last_ref[i] = jnp.broadcast_to(seg[i : i + 1, GROUP - 1 :], (1, HEAD))
    own_rate = rate_ref[me // RING]
    keep = jnp.exp(jnp.zeros((8, HEAD), F32) - own_rate * GROUP)
    joined = (step_seg_b == step_seg_e) | (steps == 0)
    carry_ref[...] = jnp.where(joined, keep, 0.0)
    carry_copy = pltpu.make_async_copy(carry_ref, carry_s, smem_sem.at[0])
    carry_copy.start()

    pl.semaphore_wait(barrier, others + sides - 1)
    for peer in peers:
        pltpu.make_async_remote_copy(
            src_ref=hmine_ref, dst_ref=hall_ref.at[me], send_sem=hsend, recv_sem=hrecv,
            device_id=(peer, side), device_id_type=MESH,
        ).start()

    def rows_of(i):
        return pl.ds(pl.multiple_of(i * GROUP, GROUP), GROUP)

    def scatter_chunk(got_ref, c, send_sem, recv_sem):
        for peer in peers:
            pltpu.make_async_remote_copy(
                src_ref=send_ref.at[peer, pl.ds(c * CHUNK, CHUNK)],
                dst_ref=got_ref.at[pl.ds(me * groups + c * CHUNK, CHUNK)],
                send_sem=send_sem, recv_sem=recv_sem,
                device_id=(peer, side), device_id_type=MESH,
            ).start()

    def return_chunk(dst_ref, c, send_sem, recv_sem):
        for peer in peers:
            pltpu.make_async_remote_copy(
                src_ref=back_ref.at[pl.ds(peer * groups + c * CHUNK, CHUNK)],
                dst_ref=dst_ref.at[me, pl.ds(c * CHUNK, CHUNK)],
                send_sem=send_sem, recv_sem=recv_sem.at[c],
                device_id=(peer, side), device_id_type=MESH,
            ).start()

    def own_slice(got_ref, n):
        return pltpu.make_async_copy(send_ref.at[me], got_ref.at[pl.ds(me * groups, groups)], own_sem.at[n])

    def own_back(dst_ref, n):
        return pltpu.make_async_copy(back_ref.at[pl.ds(me * groups, groups)], dst_ref.at[me], own_sem.at[n])

    def store_state(i, h, s):
        send_ref[RING * h : RING * (h + 1), i] = s.astype(BF16).reshape(RING, part, HEAD)

    def state_of(ref, i, h):
        return ref[RING * h : RING * (h + 1), i].reshape(HEAD, HEAD)

    def summary_group(i, _):
        rows = rows_of(i)
        seg_c = jnp.broadcast_to(segr_ref[i], (GROUP, GROUP)).T
        segc_ref[i] = seg_c
        live = seg_c == last_ref[i]
        for h in range(heads):
            cols = cols_of(h)
            w = (jnp.where(live, kdec_ref[h], 0.0) * v_ref[rows, cols].astype(F32)).astype(BF16)
            store_state(i, h, dot(k_ref[rows, cols], w, TN))
        return 0

    def summary_chunk(c, _):
        slab_copy(k_hbm, k_ref, c, kv_sem.at[0, c]).wait()
        slab_copy(v_hbm, v_ref, c, kv_sem.at[1, c]).wait()
        lax.fori_loop(c * CHUNK, (c + 1) * CHUNK, summary_group, 0)
        scatter_chunk(got1_ref, c, send1, recv1)
        return 0

    lax.fori_loop(0, chunks, summary_chunk, 0)
    own_slice(got1_ref, 0).start()

    wait_bytes(hall_ref.at[pl.ds(0, others)], hrecv)
    for d in range(devices):
        hcomp_ref[d : d + 1] = hall_ref[d, 0:1]
    homes_copy = pltpu.make_async_copy(hcomp_ref, homes_s, smem_sem.at[1])
    homes_copy.start()
    homes_copy.wait()

    def invert(b, acc):
        for n in range(UNROLL):
            p = b * UNROLL + n
            acc = jnp.where(steps == homes_s[p // groups, lax.rem(p, groups)], p, acc)
        return acc

    order_ref[...] = lax.fori_loop(0, total // UNROLL, invert, jnp.zeros((8, HEAD), I32))
    order_copy = pltpu.make_async_copy(order_ref, order_s, smem_sem.at[2])
    order_copy.start()
    load_q.wait()
    load_u.wait()

    def inner_group(i, _):
        rows = rows_of(i)
        same = segc_ref[i] == segr_ref[i]
        for h in range(heads):
            cols = cols_of(h)
            scores = dot(q_ref[rows, cols], k_ref[rows, cols], NT)
            mixing = (scores * jnp.where(same, dec_ref[h], 0.0)).astype(BF16)
            mix_ref[i * heads + h] = mixing
            att_ref[rows, cols] = dot(mixing, v_ref[rows, cols], NN)
        return 0

    lax.fori_loop(0, groups, inner_group, 0)
    order_copy.wait()
    carry_copy.wait()

    def scan(got_ref, reverse):
        def step(b, state):
            b = total // UNROLL - 1 - b if reverse else b
            for n in range(UNROLL):
                t = b * UNROLL + (UNROLL - 1 - n if reverse else n)
                hi, lo = t // HEAD, lax.rem(t, HEAD)
                seq_ref[t] = state.astype(BF16)
                state = carry_s[hi, lo] * state + got_ref[order_s[hi, lo]].astype(F32)
            return state

        lax.fori_loop(0, total // UNROLL, step, jnp.zeros((part, HEAD), F32))

        def put(b, _):
            for n in range(UNROLL):
                p = b * UNROLL + n
                back_ref[p] = seq_ref[homes_s[p // groups, lax.rem(p, groups)]]
            return 0

        lax.fori_loop(0, total // UNROLL, put, 0)

    own_slice(got1_ref, 0).wait()
    wait_bytes(got1_ref.at[pl.ds(0, others * groups)], recv1)
    scan(got1_ref, False)

    def return_all(dst_ref, send_sem, recv_sem):
        def body(c, _):
            return_chunk(dst_ref, c, send_sem, recv_sem)
            return 0

        lax.fori_loop(0, chunks, body, 0)

    return_all(prev_ref, send2, recv2)
    own_back(prev_ref, 1).start()
    wait_bytes(send_ref.at[pl.ds(0, others)], send1)
    wait_bytes(hall_ref.at[pl.ds(0, others)], hsend)
    own_back(prev_ref, 1).wait()

    lane = iota((GROUP, HEAD), 1)
    pieces = GROUP // (2 * CHUNK)
    width = 2 * CHUNK

    def output_group(c, g, acc):
        i = c * CHUNK + g
        rows = rows_of(i)
        live = segc_ref[i] == bef_ref[i]
        squares = jnp.zeros((GROUP, HEAD), F32)
        crossed = jnp.zeros((GROUP, HEAD), F32)
        for h in range(heads):
            cols = cols_of(h)
            carried = dot(q_ref[rows, cols], state_of(prev_ref, i, h), NN)
            out = att_ref[rows, cols] + jnp.where(live, qdec_ref[h], 0.0) * carried
            att_ref[rows, cols] = out
            squares += out * out
            crossed += gain_ref[:, cols] * u_ref[rows, cols].astype(F32) * out
        squares = jnp.sum(squares, axis=1, keepdims=True)
        crossed = jnp.sum(crossed, axis=1, keepdims=True)
        return jnp.where(lane == g, squares, jnp.where(lane == g + CHUNK, crossed, acc))

    def total_copy(c, n):
        return pltpu.make_async_remote_copy(
            src_ref=mine_ref.at[c], dst_ref=gsum_ref.at[c, n], send_sem=ssend.at[c], recv_sem=srecv.at[c],
            device_id=(me, mates[n]), device_id_type=MESH,
        )

    def output_chunk(c):
        wait_bytes(prev_ref.at[pl.ds(0, others), pl.ds(c * CHUNK, CHUNK)], recv2.at[c])
        acc = lax.fori_loop(0, CHUNK, functools.partial(output_group, c), jnp.zeros((GROUP, HEAD), F32))
        packed = acc[0:width]
        for n in range(1, pieces):
            packed += pltpu.roll(acc[n * width : (n + 1) * width], n * width, 1)
        mine_ref[c] = packed
        for n in range(sides - 1):
            total_copy(c, n).start()

    channels = heads * HEAD * sides

    def cotangent_group(c, sums, g, _):
        i = c * CHUNK + g
        rows = rows_of(i)
        live = segc_ref[i] == bef_ref[i]
        squares = jnp.sum(jnp.where(lane == g, sums, 0.0), axis=1, keepdims=True)
        crossed = jnp.sum(jnp.where(lane == g + CHUNK, sums, 0.0), axis=1, keepdims=True)
        scaling = lax.rsqrt(squares / channels + EPSILON)
        pull = scaling * scaling * scaling * (crossed / channels)
        for h in range(heads):
            cols = cols_of(h)
            wide = gain_ref[:, cols] * u_ref[rows, cols].astype(F32)
            grad = (scaling * wide - pull * att_ref[rows, cols]).astype(BF16)
            u_ref[rows, cols] = grad
            w = (jnp.where(live, qdec_ref[h], 0.0) * grad.astype(F32)).astype(BF16)
            store_state(i, h, dot(q_ref[rows, cols], w, TN))
        return 0

    def cotangent_chunk(c):
        wait_bytes(gsum_ref.at[c], srecv.at[c])
        wait_bytes(gsum_ref.at[c], ssend.at[c])
        both = mine_ref[c]
        for n in range(sides - 1):
            both += gsum_ref[c, n]
        sums = jnp.concatenate(
            [both] + [pltpu.roll(both, HEAD - n * width, 1) for n in range(1, pieces)], axis=0
        )
        lax.fori_loop(0, CHUNK, functools.partial(cotangent_group, c, sums), 0)
        scatter_chunk(got2_ref, c, send3, recv3)

    def middle(c, _):
        @pl.when(c < chunks)
        def _():
            output_chunk(c)

        @pl.when(c >= 1)
        def _():
            cotangent_chunk(c - 1)

        return 0

    lax.fori_loop(0, chunks + 1, middle, 0)
    own_slice(got2_ref, 2).start()

    def local_group(i, _):
        rows = rows_of(i)
        seg_c = segc_ref[i]
        same = seg_c == segr_ref[i]
        live = seg_c == bef_ref[i]
        for h in range(heads):
            cols = cols_of(h)
            g, k, q = u_ref[rows, cols], k_ref[rows, cols], q_ref[rows, cols]
            score = (dot(g, v_ref[rows, cols], NT) * jnp.where(same, dec_ref[h], 0.0)).astype(BF16)
            carried = jnp.where(live, qdec_ref[h], 0.0) * dot(g, state_of(prev_ref, i, h), NT)
            qout_ref[rows, cols] = (dot(score, k, NN) + carried).astype(BF16)
            att_ref[rows, cols] = dot(score, q, TN)
            vgp_ref[rows, cols] = dot(mix_ref[i * heads + h], g, TN)
        return 0

    early = groups // 2
    lax.fori_loop(0, early, local_group, 0)
    for c in range(chunks):
        wait_bytes(prev_ref.at[pl.ds(0, others), pl.ds(0, CHUNK)], send2)
    own_slice(got2_ref, 2).wait()
    wait_bytes(got2_ref.at[pl.ds(0, others * groups)], recv3)
    scan(got2_ref, True)
    return_all(after_ref, send4, recv4)
    own_back(after_ref, 3).start()
    lax.fori_loop(early, groups, local_group, 0)
    store_q = pltpu.make_async_copy(qout_ref, qo_hbm, out_sem.at[2, 0])
    store_q.start()
    own_back(after_ref, 3).wait()

    def final_group(i, _):
        rows = rows_of(i)
        live = segc_ref[i] == last_ref[i]
        for h in range(heads):
            cols = cols_of(h)
            after = state_of(after_ref, i, h)
            w = jnp.where(live, kdec_ref[h], 0.0)
            kout_ref[rows, cols] = (att_ref[rows, cols] + w * dot(v_ref[rows, cols], after, NT)).astype(BF16)
            vout_ref[rows, cols] = (vgp_ref[rows, cols] + w * dot(k_ref[rows, cols], after, NN)).astype(BF16)
        return 0

    def final_chunk(c, _):
        wait_bytes(after_ref.at[pl.ds(0, others), pl.ds(c * CHUNK, CHUNK)], recv4.at[c])
        lax.fori_loop(c * CHUNK, (c + 1) * CHUNK, final_group, 0)
        rows = pl.ds(c * slab, slab)
        pltpu.make_async_copy(kout_ref.at[rows], ko_hbm.at[rows], out_sem.at[0, c]).start()
        pltpu.make_async_copy(vout_ref.at[rows], vo_hbm.at[rows], out_sem.at[1, c]).start()
        return 0

    lax.fori_loop(0, chunks, final_chunk, 0)
    store_q.wait()
    for c in range(chunks):
        rows = pl.ds(c * slab, slab)
        pltpu.make_async_copy(kout_ref.at[rows], ko_hbm.at[rows], out_sem.at[0, c]).wait()
        pltpu.make_async_copy(vout_ref.at[rows], vo_hbm.at[rows], out_sem.at[1, c]).wait()
    wait_bytes(send_ref.at[pl.ds(0, others)], send3)
    wait_bytes(send_ref.at[pl.ds(0, others)], send4)


def shards(q, k, v, u, gain, rate, lengths, home):
    devices = lax.axis_size("seq")
    sides = lax.axis_size("head")
    heads = q.shape[1] // HEAD
    groups = home.shape[0]
    rows, width = q.shape
    docs = lengths.shape[0]
    total = devices * groups
    chunks = groups // CHUNK
    part = HEAD // RING
    smem = pl.BlockSpec(memory_space=pltpu.SMEM)
    any_ = pl.BlockSpec(memory_space=pl.ANY)
    vmem, dma = pltpu.VMEM, pltpu.SemaphoreType.DMA
    table = vmem((heads, GROUP, GROUP), F32)
    strip = vmem((groups, 1, HEAD), F32)
    token = vmem((rows, width), BF16)
    flat = vmem((total, part, HEAD), BF16)
    state = vmem((devices, groups, part, HEAD), BF16)
    wide = vmem((rows, width), F32)
    scratch = (
        [token] * 4 + [state, flat, flat, flat, flat, state, state]
        + [wide, wide, vmem((groups * heads, GROUP, GROUP), BF16)] + [token] * 3
        + [table] * 3 + [strip] * 3 + [vmem((groups, GROUP, GROUP), F32)]
        + [vmem((8, HEAD), I32), vmem((devices, 8, HEAD), I32), vmem((devices, HEAD), I32)]
        + [vmem((8, HEAD), I32), vmem((8, HEAD), F32)]
        + [pltpu.SMEM((devices, HEAD), I32), pltpu.SMEM((8, HEAD), I32), pltpu.SMEM((8, HEAD), F32)]
        + [vmem((chunks, 2 * CHUNK, HEAD), F32), vmem((chunks, sides - 1, 2 * CHUNK, HEAD), F32)]
        + [dma((2, chunks)), dma((2,)), dma((4,)), dma((3,)), dma, dma, dma, dma, dma, dma((chunks,))]
        + [dma, dma, dma, dma((chunks,)), dma((chunks,)), dma((chunks,)), dma((3, chunks))]
    )
    return pl.pallas_call(
        functools.partial(fused_kernel, heads, groups, devices, sides, docs),
        out_shape=(jax.ShapeDtypeStruct((rows, width), BF16),) * 3,
        in_specs=[smem, smem, smem, pl.BlockSpec(memory_space=vmem)] + [any_] * 4,
        out_specs=(any_,) * 3,
        scratch_shapes=scratch,
        compiler_params=pltpu.CompilerParams(
            collective_id=0, has_side_effects=True, vmem_limit_bytes=52 << 20
        ),
    )(rate, lengths, home, gain.reshape(1, width), q, k, v, u)


def solution(mesh):
    rows = P("seq", "head")
    return jax.shard_map(
        shards,
        mesh=mesh,
        in_specs=(rows, rows, rows, rows, P("head"), P("head"), P(), P("seq")),
        out_specs=(rows, rows, rows),
        check_vma=False,
    )
```

time: 712 us -> 129 us (0.18)
  waiting for transfers between devices: 243 us -> 0 us
  blocking collectives: 136 us -> 0 us
  starting transfers between devices: 128 us -> 0 us
  Pallas kernels: 0 us -> 118 us
  local copies, waits for them, and re-layouts: 119 us -> 9.5 us
  matrix products: 41.3 us -> 0 us
  other arithmetic: 35 us -> 0 us
    ppermute x30 -> x0, waiting for transfers between devices: 161 us -> none  [from_behind(): return lax.ppermute(block, axis, route)]
    pallas_call x0 -> x1, Pallas kernels: none -> 118 us  [shards(): pl.pallas_call(functools.partial(fused_kernel, heads, groups, devices, si...]
    all_to_all x3 -> x0, blocking collectives: 113 us -> none  [the longest x1 42.8 us: shards(): lax.all_to_all(homeward(value_grad), 'seq', split_axis=0, concat_axis=0,...]
    ppermute x30 -> x0, starting transfers between devices: 102 us -> none  [from_behind(): return lax.ppermute(block, axis, route)]
    all_to_all x5 -> x0, waiting for transfers between devices: 81.4 us -> none  [the longest x1 27.3 us: shards(): lax.all_to_all(outgoing(query_rows), 'seq', split_axis=0, concat_axis=0,...]
    gather x15 -> x0, local copies, waits for them, and re-layouts: 49 us -> none  [the longest x4 13.7 us: outgoing(): return jnp.take(rows.reshape(group_shape), picked, axis=0)]
    dot_general x12 -> x0, matrix products: 41.3 us -> none  [the longest x1 7.6 us: output_local(): jnp.einsum('cjhd,chde->cjhe', query_c, prev_states, preferred_element_typ...]
    reshape x9 -> x0, local copies, waits for them, and re-layouts: 26.6 us -> none  [the longest x8 23.7 us: outgoing(): return jnp.take(rows.reshape(group_shape), picked, axis=0)]
  transfers between devices with their start and end apart: 35 -> 0, of which waited for: 34 -> 0; matrix products, arithmetic and copies ran while one was open for 9% -> 0% of each run, Pallas kernels for 0% -> 0%
where the time goes in v2:
time: 129 us
  Pallas kernels  118 us (91%)
  local copies, waits for them, and re-layouts  9.5 us (7%)
    pallas_call x1, Pallas kernels, shards(): pl.pallas_call(functools.partial(fused_kernel, heads, groups, devices, si...  118 us
    unnamed x15, local copies, waits for them, and re-layouts  9.5 us

profile of v2, /device:TPU:0, one launch (start us, length us, event | category | flops | bytes accessed | tf_op | source)
XLA Modules:
  0.0 128.5 jit_solution(4903745947629722882)
XLA Ops:
  0.6 0.0 copy-start
  0.6 0.7 copy-done
  1.3 0.0 copy-start.1
  1.3 0.7 copy-done.1
  2.0 0.0 copy-start.2
  2.0 0.7 copy-done.2
  2.6 0.0 copy-start.3
  2.6 0.7 copy-done.3
  3.3 118.4 %shard_map.103 = (bf16[2048,512]{1,0:T(8,128)(2,1)}, bf16[2048,512]{1,0:T(8,128)(2,1)}, bf16[2048,512]{1,0:T(8,128)(2,1)}) custom-call(f32[4]{0:T(128)S(1)} %copy-done.1, s32[32]{0:T(128)S(1)} %copy-done.2, s32[16]{0:T(128)S(1)} %copy-done.3, f32[1,512]{1,0:T(1,128)S(1)} %bitcast.1, bf16[2048,512]{1,0:T(8,128)(2,1)} %q_hbm.1, bf16[2048,512]{1,0:T(8,128)(2,1)} %k_hbm.1, ...), custom_call_target="tpu_custom_call" | custom-call | tf_op jit(solution)/shard_map/pallas_call | solution.py:434
  121.6 0.0 copy-start.5
  121.7 3.2 %copy.14 = bf16[2048,512]{1,0:T(8,128)(2,1)} copy(bf16[2048,512]{1,0:T(8,128)(2,1)} %get-tuple-element.6) | data formatting | bytes 4194304
  124.8 0.0 copy-done.5
  124.9 0.0 copy-start.4
  124.9 1.3 %copy.15 = bf16[2048,512]{1,0:T(8,128)(2,1)} copy(bf16[2048,512]{1,0:T(8,128)(2,1)S(1)} %copy-done.5) | data formatting | bytes 4194304
  126.2 1.0 copy-done.4
  127.2 1.3 %copy.16 = bf16[2048,512]{1,0:T(8,128)(2,1)} copy(bf16[2048,512]{1,0:T(8,128)(2,1)S(1)} %copy-done.4) | data formatting | bytes 4194304
Async XLA Ops:
  0.6 0.7 copy-start
  1.3 0.7 copy-start.1
  2.0 0.7 copy-start.2
  2.6 0.7 copy-start.3
  121.6 3.2 %copy-start.5 = (bf16[2048,512]{1,0:T(8,128)(2,1)S(1)}, bf16[2048,512]{1,0:T(8,128)(2,1)}, u32[]{:S(2)}) copy-start(bf16[2048,512]{1,0:T(8,128)(2,1)} %get-tuple-element.7) | copy-start | bytes 6291460
  124.9 2.3 %copy-start.4 = (bf16[2048,512]{1,0:T(8,128)(2,1)S(1)}, bf16[2048,512]{1,0:T(8,128)(2,1)}, u32[]{:S(2)}) copy-start(bf16[2048,512]{1,0:T(8,128)(2,1)} %get-tuple-element.8) | copy-start | bytes 6291460

commit v3 on v2

--- a/solution.py
+++ b/solution.py
@@ -47,24 +47,25 @@
     heads, groups, devices, sides, docs,
     rate_ref, len_ref, home_ref, gain_ref, q_hbm, k_hbm, v_hbm, u_hbm,
     qo_hbm, ko_hbm, vo_hbm,
-    q_ref, k_ref, v_ref, u_ref, send_ref, got1_ref, got2_ref, seq_ref, back_ref, prev_ref, after_ref,
+    q_ref, k_ref, v_ref, u_ref, send_ref, got1a_ref, got1b_ref, got2a_ref, got2b_ref, seq_ref, back_ref, prev_ref, after_ref,
     att_ref, vgp_ref, mix_ref, qout_ref, kout_ref, vout_ref,
     dec_ref, qdec_ref, kdec_ref, segr_ref, bef_ref, last_ref, segc_ref,
     hmine_ref, hall_ref, hcomp_ref, order_ref, carry_ref, homes_s, order_s, carry_s,
     mine_ref, gsum_ref,
-    kv_sem, qu_sem, own_sem, smem_sem, hsend, hrecv, send1, recv1, send2, recv2,
-    send3, recv3, send4, recv4, ssend, srecv, out_sem,
+    kv_sem, qu_sem, own_sem, smem_sem, hsend, hrecv, send1, recv1, send2, recv2a, recv2b,
+    send3, recv3, send4, recv4a, recv4b, ssend, srecv, out_sem,
 ):
     me = lax.axis_index("seq")
     side = lax.axis_index("head")
     y, z = me // RING, lax.rem(me, RING)
     peers = [lax.rem(y + dy, RING) * RING + lax.rem(z + dz, RING) for dy, dz in torus_offsets(RING)]
     mates = [lax.rem(side + n, sides) for n in range(1, sides)]
+    got1_ref, got2_ref = (got1a_ref, got1b_ref), (got2a_ref, got2b_ref)
     others = devices - 1
     total = devices * groups
     chunks = groups // CHUNK
     slab = CHUNK * GROUP
-    part = HEAD // RING
+    part = HEAD // RING // 2
 
     barrier = pltpu.get_barrier_semaphore()
     for peer in peers:
@@ -139,35 +140,39 @@
     def rows_of(i):
         return pl.ds(pl.multiple_of(i * GROUP, GROUP), GROUP)
 
-    def scatter_chunk(got_ref, c, send_sem, recv_sem):
+    def scatter(got_ref, half, c, send_sem, recv_sem):
         for peer in peers:
             pltpu.make_async_remote_copy(
-                src_ref=send_ref.at[peer, pl.ds(c * CHUNK, CHUNK)],
-                dst_ref=got_ref.at[pl.ds(me * groups + c * CHUNK, CHUNK)],
+                src_ref=send_ref.at[half, peer, pl.ds(c * CHUNK, CHUNK)],
+                dst_ref=got_ref[half].at[pl.ds(me * groups + c * CHUNK, CHUNK)],
+                send_sem=send_sem, recv_sem=recv_sem.at[half],
+                device_id=(peer, side), device_id_type=MESH,
+            ).start()
+
+    def give_back(dst_ref, half, start, size, send_sem, recv_sem):
+        for peer in peers:
+            pltpu.make_async_remote_copy(
+                src_ref=back_ref.at[half, pl.ds(peer * groups + start, size)],
+                dst_ref=dst_ref.at[half, me, pl.ds(start, size)],
                 send_sem=send_sem, recv_sem=recv_sem,
                 device_id=(peer, side), device_id_type=MESH,
             ).start()
 
-    def return_chunk(dst_ref, c, send_sem, recv_sem):
-        for peer in peers:
-            pltpu.make_async_remote_copy(
-                src_ref=back_ref.at[pl.ds(peer * groups + c * CHUNK, CHUNK)],
-                dst_ref=dst_ref.at[me, pl.ds(c * CHUNK, CHUNK)],
-                send_sem=send_sem, recv_sem=recv_sem.at[c],
-                device_id=(peer, side), device_id_type=MESH,
-            ).start()
-
-    def own_slice(got_ref, n):
-        return pltpu.make_async_copy(send_ref.at[me], got_ref.at[pl.ds(me * groups, groups)], own_sem.at[n])
-
-    def own_back(dst_ref, n):
-        return pltpu.make_async_copy(back_ref.at[pl.ds(me * groups, groups)], dst_ref.at[me], own_sem.at[n])
+    def own_slice(got_ref, half, n):
+        return pltpu.make_async_copy(
+            send_ref.at[half, me], got_ref[half].at[pl.ds(me * groups, groups)], own_sem.at[n, half]
+        )
+
+    def own_back(dst_ref, half, n):
+        return pltpu.make_async_copy(
+            back_ref.at[half, pl.ds(me * groups, groups)], dst_ref.at[half, me], own_sem.at[n, half]
+        )
 
     def store_state(i, h, s):
-        send_ref[RING * h : RING * (h + 1), i] = s.astype(BF16).reshape(RING, part, HEAD)
+        send_ref[:, RING * h : RING * (h + 1), i] = s.astype(BF16).reshape(2, RING, part, HEAD)
 
     def state_of(ref, i, h):
-        return ref[RING * h : RING * (h + 1), i].reshape(HEAD, HEAD)
+        return ref[:, RING * h : RING * (h + 1), i].reshape(HEAD, HEAD)
 
     def summary_group(i, _):
         rows = rows_of(i)
@@ -184,11 +189,18 @@
         slab_copy(k_hbm, k_ref, c, kv_sem.at[0, c]).wait()
         slab_copy(v_hbm, v_ref, c, kv_sem.at[1, c]).wait()
         lax.fori_loop(c * CHUNK, (c + 1) * CHUNK, summary_group, 0)
-        scatter_chunk(got1_ref, c, send1, recv1)
+        scatter(got1_ref, 0, c, send1, recv1)
         return 0
 
     lax.fori_loop(0, chunks, summary_chunk, 0)
-    own_slice(got1_ref, 0).start()
+
+    def second_half(c, _):
+        scatter(got1_ref, 1, c, send1, recv1)
+        return 0
+
+    lax.fori_loop(0, chunks, second_half, 0)
+    own_slice(got1_ref, 0, 0).start()
+    own_slice(got1_ref, 1, 0).start()
 
     wait_bytes(hall_ref.at[pl.ds(0, others)], hrecv)
     for d in range(devices):
@@ -224,14 +236,14 @@
     order_copy.wait()
     carry_copy.wait()
 
-    def scan(got_ref, reverse):
+    def scan(got_ref, half, reverse):
         def step(b, state):
             b = total // UNROLL - 1 - b if reverse else b
             for n in range(UNROLL):
                 t = b * UNROLL + (UNROLL - 1 - n if reverse else n)
                 hi, lo = t // HEAD, lax.rem(t, HEAD)
                 seq_ref[t] = state.astype(BF16)
-                state = carry_s[hi, lo] * state + got_ref[order_s[hi, lo]].astype(F32)
+                state = carry_s[hi, lo] * state + got_ref[half][order_s[hi, lo]].astype(F32)
             return state
 
         lax.fori_loop(0, total // UNROLL, step, jnp.zeros((part, HEAD), F32))
@@ -239,27 +251,52 @@
         def put(b, _):
             for n in range(UNROLL):
                 p = b * UNROLL + n
-                back_ref[p] = seq_ref[homes_s[p // groups, lax.rem(p, groups)]]
+                back_ref[half, p] = seq_ref[homes_s[p // groups, lax.rem(p, groups)]]
             return 0
 
         lax.fori_loop(0, total // UNROLL, put, 0)
 
-    own_slice(got1_ref, 0).wait()
-    wait_bytes(got1_ref.at[pl.ds(0, others * groups)], recv1)
-    scan(got1_ref, False)
-
-    def return_all(dst_ref, send_sem, recv_sem):
-        def body(c, _):
-            return_chunk(dst_ref, c, send_sem, recv_sem)
+    half_groups = groups // 2
+
+    def turn(got_ref, dst_ref, n, reverse, recv_sem, send_back, recv_first, recv_second):
+        own_slice(got_ref, 0, n).wait()
+        wait_bytes(got_ref[0].at[pl.ds(0, others * groups)], recv_sem.at[0])
+        scan(got_ref, 0, reverse)
+        give_back(dst_ref, 0, 0, half_groups, send_back, recv_first.at[0])
+        own_back(dst_ref, 0, n + 1).start()
+        own_slice(got_ref, 1, n).wait()
+        wait_bytes(got_ref[1].at[pl.ds(0, others * groups)], recv_sem.at[1])
+        scan(got_ref, 1, reverse)
+        own_back(dst_ref, 1, n + 1).start()
+
+        def rest(c, _):
+            @pl.when(c == chunks // 2)
+            def _():
+                give_back(dst_ref, 0, half_groups, half_groups, send_back, recv_first.at[1])
+
+            give_back(dst_ref, 1, c * CHUNK, CHUNK, send_back, recv_second.at[c])
             return 0
 
-        lax.fori_loop(0, chunks, body, 0)
-
-    return_all(prev_ref, send2, recv2)
-    own_back(prev_ref, 1).start()
-    wait_bytes(send_ref.at[pl.ds(0, others)], send1)
+        lax.fori_loop(0, chunks, rest, 0)
+
+    def turned(dst_ref, c, recv_first, recv_second):
+        @pl.when(lax.rem(c, chunks // 2) == 0)
+        def _():
+            wait_bytes(
+                dst_ref.at[0, pl.ds(0, others), pl.ds(0, half_groups)], recv_first.at[c // (chunks // 2)]
+            )
+
+        wait_bytes(dst_ref.at[1, pl.ds(0, others), pl.ds(0, CHUNK)], recv_second.at[c])
+
+    def sent(sem):
+        wait_bytes(send_ref.at[0, pl.ds(0, others)], sem)
+        wait_bytes(send_ref.at[0, pl.ds(0, others)], sem)
+
+    turn(got1_ref, prev_ref, 0, False, recv1, send2, recv2a, recv2b)
+    sent(send1)
     wait_bytes(hall_ref.at[pl.ds(0, others)], hsend)
-    own_back(prev_ref, 1).wait()
+    own_back(prev_ref, 0, 1).wait()
+    own_back(prev_ref, 1, 1).wait()
 
     lane = iota((GROUP, HEAD), 1)
     pieces = GROUP // (2 * CHUNK)
@@ -289,7 +326,7 @@
         )
 
     def output_chunk(c):
-        wait_bytes(prev_ref.at[pl.ds(0, others), pl.ds(c * CHUNK, CHUNK)], recv2.at[c])
+        turned(prev_ref, c, recv2a, recv2b)
         acc = lax.fori_loop(0, CHUNK, functools.partial(output_group, c), jnp.zeros((GROUP, HEAD), F32))
         packed = acc[0:width]
         for n in range(1, pieces):
@@ -327,7 +364,11 @@
             [both] + [pltpu.roll(both, HEAD - n * width, 1) for n in range(1, pieces)], axis=0
         )
         lax.fori_loop(0, CHUNK, functools.partial(cotangent_group, c, sums), 0)
-        scatter_chunk(got2_ref, c, send3, recv3)
+        scatter(got2_ref, 0, c, send3, recv3)
+
+        @pl.when(c < chunks - 2)
+        def _():
+            scatter(got2_ref, 1, c, send3, recv3)
 
     def middle(c, _):
         @pl.when(c < chunks)
@@ -341,7 +382,10 @@
         return 0
 
     lax.fori_loop(0, chunks + 1, middle, 0)
-    own_slice(got2_ref, 2).start()
+    for c in (chunks - 2, chunks - 1):
+        scatter(got2_ref, 1, c, send3, recv3)
+    own_slice(got2_ref, 0, 2).start()
+    own_slice(got2_ref, 1, 2).start()
 
     def local_group(i, _):
         rows = rows_of(i)
@@ -360,17 +404,13 @@
 
     early = groups // 2
     lax.fori_loop(0, early, local_group, 0)
-    for c in range(chunks):
-        wait_bytes(prev_ref.at[pl.ds(0, others), pl.ds(0, CHUNK)], send2)
-    own_slice(got2_ref, 2).wait()
-    wait_bytes(got2_ref.at[pl.ds(0, others * groups)], recv3)
-    scan(got2_ref, True)
-    return_all(after_ref, send4, recv4)
-    own_back(after_ref, 3).start()
+    sent(send2)
+    turn(got2_ref, after_ref, 2, True, recv3, send4, recv4a, recv4b)
     lax.fori_loop(early, groups, local_group, 0)
     store_q = pltpu.make_async_copy(qout_ref, qo_hbm, out_sem.at[2, 0])
     store_q.start()
-    own_back(after_ref, 3).wait()
+    own_back(after_ref, 0, 3).wait()
+    own_back(after_ref, 1, 3).wait()
 
     def final_group(i, _):
         rows = rows_of(i)
@@ -384,7 +424,7 @@
         return 0
 
     def final_chunk(c, _):
-        wait_bytes(after_ref.at[pl.ds(0, others), pl.ds(c * CHUNK, CHUNK)], recv4.at[c])
+        turned(after_ref, c, recv4a, recv4b)
         lax.fori_loop(c * CHUNK, (c + 1) * CHUNK, final_group, 0)
         rows = pl.ds(c * slab, slab)
         pltpu.make_async_copy(kout_ref.at[rows], ko_hbm.at[rows], out_sem.at[0, c]).start()
@@ -397,8 +437,8 @@
         rows = pl.ds(c * slab, slab)
         pltpu.make_async_copy(kout_ref.at[rows], ko_hbm.at[rows], out_sem.at[0, c]).wait()
         pltpu.make_async_copy(vout_ref.at[rows], vo_hbm.at[rows], out_sem.at[1, c]).wait()
-    wait_bytes(send_ref.at[pl.ds(0, others)], send3)
-    wait_bytes(send_ref.at[pl.ds(0, others)], send4)
+    sent(send3)
+    sent(send4)
 
 
 def shards(q, k, v, u, gain, rate, lengths, home):
@@ -410,7 +450,7 @@
     docs = lengths.shape[0]
     total = devices * groups
     chunks = groups // CHUNK
-    part = HEAD // RING
+    part = HEAD // RING // 2
     smem = pl.BlockSpec(memory_space=pltpu.SMEM)
     any_ = pl.BlockSpec(memory_space=pl.ANY)
     vmem, dma = pltpu.VMEM, pltpu.SemaphoreType.DMA
@@ -418,18 +458,19 @@
     strip = vmem((groups, 1, HEAD), F32)
     token = vmem((rows, width), BF16)
     flat = vmem((total, part, HEAD), BF16)
-    state = vmem((devices, groups, part, HEAD), BF16)
+    state = vmem((2, devices, groups, part, HEAD), BF16)
     wide = vmem((rows, width), F32)
     scratch = (
-        [token] * 4 + [state, flat, flat, flat, flat, state, state]
+        [token] * 4 + [state] + [flat] * 5 + [vmem((2, total, part, HEAD), BF16), state, state]
         + [wide, wide, vmem((groups * heads, GROUP, GROUP), BF16)] + [token] * 3
         + [table] * 3 + [strip] * 3 + [vmem((groups, GROUP, GROUP), F32)]
         + [vmem((8, HEAD), I32), vmem((devices, 8, HEAD), I32), vmem((devices, HEAD), I32)]
         + [vmem((8, HEAD), I32), vmem((8, HEAD), F32)]
         + [pltpu.SMEM((devices, HEAD), I32), pltpu.SMEM((8, HEAD), I32), pltpu.SMEM((8, HEAD), F32)]
         + [vmem((chunks, 2 * CHUNK, HEAD), F32), vmem((chunks, sides - 1, 2 * CHUNK, HEAD), F32)]
-        + [dma((2, chunks)), dma((2,)), dma((4,)), dma((3,)), dma, dma, dma, dma, dma, dma((chunks,))]
-        + [dma, dma, dma, dma((chunks,)), dma((chunks,)), dma((chunks,)), dma((3, chunks))]
+        + [dma((2, chunks)), dma((2,)), dma((4, 2)), dma((3,)), dma, dma]
+        + [dma, dma((2,)), dma, dma((2,)), dma((chunks,))] * 2
+        + [dma((chunks,)), dma((chunks,)), dma((3, chunks))]
     )
     return pl.pallas_call(
         functools.partial(fused_kernel, heads, groups, devices, sides, docs),

time: 129 us -> 119 us (0.922)
  Pallas kernels: 118 us -> 109 us
    pallas_call x1, Pallas kernels: 118 us -> 109 us  [shards(): pl.pallas_call(functools.partial(fused_kernel, heads, groups, devices, si...]
where the time goes in v3:
time: 119 us
  Pallas kernels  109 us (92%)
  local copies, waits for them, and re-layouts  9.5 us (8%)
    pallas_call x1, Pallas kernels, shards(): pl.pallas_call(functools.partial(fused_kernel, heads, groups, devices, si...  109 us
    unnamed x15, local copies, waits for them, and re-layouts  9.5 us

profile of v3, /device:TPU:0, one launch (start us, length us, event | category | flops | bytes accessed | tf_op | source)
XLA Modules:
  0.0 118.7 jit_solution(13481883147234028550)
XLA Ops:
  0.6 0.0 copy-start
  0.6 0.7 copy-done
  1.3 0.0 copy-start.1
  1.3 0.7 copy-done.1
  2.0 0.0 copy-start.2
  2.0 0.7 copy-done.2
  2.6 0.0 copy-start.3
  2.6 0.7 copy-done.3
  3.3 108.5 %shard_map.103 = (bf16[2048,512]{1,0:T(8,128)(2,1)}, bf16[2048,512]{1,0:T(8,128)(2,1)}, bf16[2048,512]{1,0:T(8,128)(2,1)}) custom-call(f32[4]{0:T(128)S(1)} %copy-done.1, s32[32]{0:T(128)S(1)} %copy-done.2, s32[16]{0:T(128)S(1)} %copy-done.3, f32[1,512]{1,0:T(1,128)S(1)} %bitcast.1, bf16[2048,512]{1,0:T(8,128)(2,1)} %q_hbm.1, bf16[2048,512]{1,0:T(8,128)(2,1)} %k_hbm.1, ...), custom_call_target="tpu_custom_call" | custom-call | tf_op jit(solution)/shard_map/pallas_call | solution.py:475
  111.8 0.0 copy-start.5
  111.8 3.2 %copy.14 = bf16[2048,512]{1,0:T(8,128)(2,1)} copy(bf16[2048,512]{1,0:T(8,128)(2,1)} %get-tuple-element.6) | data formatting | bytes 4194304
  115.0 0.0 copy-done.5
  115.0 0.0 copy-start.4
  115.0 1.3 %copy.15 = bf16[2048,512]{1,0:T(8,128)(2,1)} copy(bf16[2048,512]{1,0:T(8,128)(2,1)S(1)} %copy-done.5) | data formatting | bytes 4194304
  116.4 1.0 copy-done.4
  117.4 1.3 %copy.16 = bf16[2048,512]{1,0:T(8,128)(2,1)} copy(bf16[2048,512]{1,0:T(8,128)(2,1)S(1)} %copy-done.4) | data formatting | bytes 4194304
Async XLA Ops:
  0.6 0.7 copy-start
  1.3 0.7 copy-start.1
  2.0 0.7 copy-start.2
  2.6 0.7 copy-start.3
  111.8 3.2 %copy-start.5 = (bf16[2048,512]{1,0:T(8,128)(2,1)S(1)}, bf16[2048,512]{1,0:T(8,128)(2,1)}, u32[]{:S(2)}) copy-start(bf16[2048,512]{1,0:T(8,128)(2,1)} %get-tuple-element.7) | copy-start | bytes 6291460
  115.0 2.3 %copy-start.4 = (bf16[2048,512]{1,0:T(8,128)(2,1)S(1)}, bf16[2048,512]{1,0:T(8,128)(2,1)}, u32[]{:S(2)}) copy-start(bf16[2048,512]{1,0:T(8,128)(2,1)} %get-tuple-element.8) | copy-start | bytes 6291460

commit v4 on v3

--- a/solution.py
+++ b/solution.py
@@ -45,15 +45,16 @@
 
 def fused_kernel(
     heads, groups, devices, sides, docs,
-    rate_ref, len_ref, home_ref, gain_ref, q_hbm, k_hbm, v_hbm, u_hbm,
-    qo_hbm, ko_hbm, vo_hbm,
+    rate_hbm, len_hbm, home_hbm, gain_hbm, q_hbm, k_hbm, v_hbm, u_hbm,
+    qout_ref, kout_ref, vout_ref,
+    rate_ref, len_ref, home_ref, gain_ref, arg_sem,
     q_ref, k_ref, v_ref, u_ref, send_ref, got1a_ref, got1b_ref, got2a_ref, got2b_ref, seq_ref, back_ref, prev_ref, after_ref,
-    att_ref, vgp_ref, mix_ref, qout_ref, kout_ref, vout_ref,
+    att_ref, vgp_ref, mix_ref,
     dec_ref, qdec_ref, kdec_ref, segr_ref, bef_ref, last_ref, segc_ref,
     hmine_ref, hall_ref, hcomp_ref, order_ref, carry_ref, homes_s, order_s, carry_s,
     mine_ref, gsum_ref,
     kv_sem, qu_sem, own_sem, smem_sem, hsend, hrecv, send1, recv1, send2, recv2a, recv2b,
-    send3, recv3, send4, recv4a, recv4b, ssend, srecv, out_sem,
+    send3, recv3, send4, recv4a, recv4b, ssend, srecv,
 ):
     me = lax.axis_index("seq")
     side = lax.axis_index("head")
@@ -67,6 +68,14 @@
     slab = CHUNK * GROUP
     part = HEAD // RING // 2
 
+    small = [
+        pltpu.make_async_copy(src, dst, arg_sem.at[n])
+        for n, (src, dst) in enumerate(
+            [(rate_hbm, rate_ref), (len_hbm, len_ref), (home_hbm, home_ref), (gain_hbm, gain_ref)]
+        )
+    ]
+    for copy in small:
+        copy.start()
     barrier = pltpu.get_barrier_semaphore()
     for peer in peers:
         pl.semaphore_signal(barrier, inc=1, device_id=(peer, side), device_id_type=MESH)
@@ -85,6 +94,8 @@
     load_q.start()
     load_u.start()
 
+    for copy in small:
+        copy.wait()
     row = iota((GROUP, GROUP), 0).astype(F32)
     spread = row - iota((GROUP, GROUP), 1).astype(F32)
     for h in range(heads):
@@ -407,8 +418,6 @@
     sent(send2)
     turn(got2_ref, after_ref, 2, True, recv3, send4, recv4a, recv4b)
     lax.fori_loop(early, groups, local_group, 0)
-    store_q = pltpu.make_async_copy(qout_ref, qo_hbm, out_sem.at[2, 0])
-    store_q.start()
     own_back(after_ref, 0, 3).wait()
     own_back(after_ref, 1, 3).wait()
 
@@ -426,19 +435,20 @@
     def final_chunk(c, _):
         turned(after_ref, c, recv4a, recv4b)
         lax.fori_loop(c * CHUNK, (c + 1) * CHUNK, final_group, 0)
-        rows = pl.ds(c * slab, slab)
-        pltpu.make_async_copy(kout_ref.at[rows], ko_hbm.at[rows], out_sem.at[0, c]).start()
-        pltpu.make_async_copy(vout_ref.at[rows], vo_hbm.at[rows], out_sem.at[1, c]).start()
         return 0
 
     lax.fori_loop(0, chunks, final_chunk, 0)
-    store_q.wait()
-    for c in range(chunks):
-        rows = pl.ds(c * slab, slab)
-        pltpu.make_async_copy(kout_ref.at[rows], ko_hbm.at[rows], out_sem.at[0, c]).wait()
-        pltpu.make_async_copy(vout_ref.at[rows], vo_hbm.at[rows], out_sem.at[1, c]).wait()
     sent(send3)
     sent(send4)
+
+
+def store_kernel(a_ref, b_ref, c_ref, ao_ref, bo_ref, co_ref, sem):
+    pairs = ((a_ref, ao_ref), (b_ref, bo_ref), (c_ref, co_ref))
+    copies = [pltpu.make_async_copy(src, dst, sem.at[n]) for n, (src, dst) in enumerate(pairs)]
+    for copy in copies:
+        copy.start()
+    for copy in copies:
+        copy.wait()
 
 
 def shards(q, k, v, u, gain, rate, lengths, home):
@@ -451,7 +461,6 @@
     total = devices * groups
     chunks = groups // CHUNK
     part = HEAD // RING // 2
-    smem = pl.BlockSpec(memory_space=pltpu.SMEM)
     any_ = pl.BlockSpec(memory_space=pl.ANY)
     vmem, dma = pltpu.VMEM, pltpu.SemaphoreType.DMA
     table = vmem((heads, GROUP, GROUP), F32)
@@ -461,8 +470,10 @@
     state = vmem((2, devices, groups, part, HEAD), BF16)
     wide = vmem((rows, width), F32)
     scratch = (
-        [token] * 4 + [state] + [flat] * 5 + [vmem((2, total, part, HEAD), BF16), state, state]
-        + [wide, wide, vmem((groups * heads, GROUP, GROUP), BF16)] + [token] * 3
+        [pltpu.SMEM((heads,), F32), pltpu.SMEM((docs,), I32), pltpu.SMEM((groups,), I32)]
+        + [vmem((1, width), F32), dma((4,))]
+        + [token] * 4 + [state] + [flat] * 5 + [vmem((2, total, part, HEAD), BF16), state, state]
+        + [wide, wide, vmem((groups * heads, GROUP, GROUP), BF16)]
         + [table] * 3 + [strip] * 3 + [vmem((groups, GROUP, GROUP), F32)]
         + [vmem((8, HEAD), I32), vmem((devices, 8, HEAD), I32), vmem((devices, HEAD), I32)]
         + [vmem((8, HEAD), I32), vmem((8, HEAD), F32)]
@@ -470,18 +481,26 @@
         + [vmem((chunks, 2 * CHUNK, HEAD), F32), vmem((chunks, sides - 1, 2 * CHUNK, HEAD), F32)]
         + [dma((2, chunks)), dma((2,)), dma((4, 2)), dma((3,)), dma, dma]
         + [dma, dma((2,)), dma, dma((2,)), dma((chunks,))] * 2
-        + [dma((chunks,)), dma((chunks,)), dma((3, chunks))]
+        + [dma((chunks,)), dma((chunks,))]
     )
-    return pl.pallas_call(
+    grads = pl.pallas_call(
         functools.partial(fused_kernel, heads, groups, devices, sides, docs),
-        out_shape=(jax.ShapeDtypeStruct((rows, width), BF16),) * 3,
-        in_specs=[smem, smem, smem, pl.BlockSpec(memory_space=vmem)] + [any_] * 4,
-        out_specs=(any_,) * 3,
+        out_shape=(pltpu.VMEM((rows, width), BF16),) * 3,
+        in_specs=[any_] * 8,
+        out_specs=(pl.BlockSpec(memory_space=vmem),) * 3,
         scratch_shapes=scratch,
         compiler_params=pltpu.CompilerParams(
-            collective_id=0, has_side_effects=True, vmem_limit_bytes=52 << 20
+            collective_id=0, has_side_effects=True, vmem_limit_bytes=50 << 20
         ),
     )(rate, lengths, home, gain.reshape(1, width), q, k, v, u)
+    return pl.pallas_call(
+        store_kernel,
+        out_shape=(jax.ShapeDtypeStruct((rows, width), BF16),) * 3,
+        in_specs=[pl.BlockSpec(memory_space=vmem)] * 3,
+        out_specs=(any_,) * 3,
+        scratch_shapes=[dma((3,))],
+        compiler_params=pltpu.CompilerParams(vmem_limit_bytes=4 << 20),
+    )(*[pltpu.with_memory_space_constraint(g, vmem) for g in grads])
 
 
 def solution(mesh):

time: 119 us -> 111 us (0.933)
  local copies, waits for them, and re-layouts: 9.5 us -> 0 us
    unnamed x15 -> x0, local copies, waits for them, and re-layouts: 9.5 us -> none
    pallas_call x0 -> x1, Pallas kernels: none -> 2.73 us  [shards(): pl.pallas_call(store_kernel, out_shape=(jax.ShapeDtypeStruct((rows, width...]
    pallas_call x1, Pallas kernels: 109 us -> 107 us  [shards(): pl.pallas_call(functools.partial(fused_kernel, heads, groups, devices, si...]
where the time goes in v4:
time: 111 us; the launch traced here: 110 us
  Pallas kernels  110 us (99%)
    pallas_call x1, Pallas kernels, shards(): pl.pallas_call(functools.partial(fused_kernel, heads, groups, devices, si...  107 us
    pallas_call x1, Pallas kernels, shards(): pl.pallas_call(store_kernel, out_shape=(jax.ShapeDtypeStruct((rows, width...  2.73 us

profile of v4, /device:TPU:0, one launch (start us, length us, event | category | flops | bytes accessed | tf_op | source)
XLA Modules:
  0.0 110.4 jit_solution(1072545000890717382)
XLA Ops:
  0.6 107.0 %shard_map.103 = (bf16[2048,512]{1,0:T(8,128)(2,1)S(1)}, bf16[2048,512]{1,0:T(8,128)(2,1)S(1)}, bf16[2048,512]{1,0:T(8,128)(2,1)S(1)}) custom-call(f32[4]{0:T(128)} %rate_hbm.1, s32[32]{0:T(128)} %len_hbm.1, s32[16]{0:T(128)} %home_hbm.1, f32[1,512]{1,0:T(1,128)} %bitcast.1, bf16[2048,512]{1,0:T(8,128)(2,1)} %q_hbm.1, bf16[2048,512]{1,0:T(8,128)(2,1)} %k_hbm.1, ...), custom_call_target="tpu_custom_call" | custom-call | tf_op jit(solution)/shard_map/pallas_call | solution.py:486
  107.7 2.7 %shard_map.104 = (bf16[2048,512]{1,0:T(8,128)(2,1)}, bf16[2048,512]{1,0:T(8,128)(2,1)}, bf16[2048,512]{1,0:T(8,128)(2,1)}) custom-call(bf16[2048,512]{1,0:T(8,128)(2,1)S(1)} %get-tuple-element.6.a_ref, bf16[2048,512]{1,0:T(8,128)(2,1)S(1)} %get-tuple-element.7.b_ref, bf16[2048,512]{1,0:T(8,128)(2,1)S(1)} %get-tuple-element.8.c_ref), custom_call_target="tpu_custom_call" | custom-call | tf_op jit(solution)/shard_map/pallas_call | solution.py:496

commit v5 on v4

--- a/solution.py
+++ b/solution.py
@@ -12,6 +12,7 @@
 RING = 4
 CHUNK = 4
 UNROLL = 8
+STEPS = 16
 EPSILON = 1e-06
 MESH = pl.DeviceIdType.MESH
 F32 = jnp.float32
@@ -91,18 +92,12 @@
         slab_copy(v_hbm, v_ref, c, kv_sem.at[1, c]).start()
     load_q = pltpu.make_async_copy(q_hbm, q_ref, qu_sem.at[0])
     load_u = pltpu.make_async_copy(u_hbm, u_ref, qu_sem.at[1])
-    load_q.start()
-    load_u.start()
 
     for copy in small:
         copy.wait()
     row = iota((GROUP, GROUP), 0).astype(F32)
-    spread = row - iota((GROUP, GROUP), 1).astype(F32)
     for h in range(heads):
-        r = rate_ref[h]
-        dec_ref[h] = jnp.where(spread >= 0.0, jnp.exp(-r * jnp.maximum(spread, 0.0)), 0.0)
-        qdec_ref[h] = jnp.exp(-r * (row + 1.0))
-        kdec_ref[h] = jnp.exp(-r * (GROUP - 1.0 - row))
+        kdec_ref[h] = jnp.exp(-rate_ref[h] * (GROUP - 1.0 - row))
 
     home_rows = jnp.zeros((groups, HEAD), I32)
     home_lanes = jnp.zeros((8, HEAD), I32)
@@ -142,11 +137,8 @@
     carry_copy.start()
 
     pl.semaphore_wait(barrier, others + sides - 1)
-    for peer in peers:
-        pltpu.make_async_remote_copy(
-            src_ref=hmine_ref, dst_ref=hall_ref.at[me], send_sem=hsend, recv_sem=hrecv,
-            device_id=(peer, side), device_id_type=MESH,
-        ).start()
+    load_q.start()
+    load_u.start()
 
     def rows_of(i):
         return pl.ds(pl.multiple_of(i * GROUP, GROUP), GROUP)
@@ -203,7 +195,13 @@
         scatter(got1_ref, 0, c, send1, recv1)
         return 0
 
-    lax.fori_loop(0, chunks, summary_chunk, 0)
+    summary_chunk(0, 0)
+    for peer in peers:
+        pltpu.make_async_remote_copy(
+            src_ref=hmine_ref, dst_ref=hall_ref.at[me], send_sem=hsend, recv_sem=hrecv,
+            device_id=(peer, side), device_id_type=MESH,
+        ).start()
+    lax.fori_loop(1, chunks, summary_chunk, 0)
 
     def second_half(c, _):
         scatter(got1_ref, 1, c, send1, recv1)
@@ -212,6 +210,12 @@
     lax.fori_loop(0, chunks, second_half, 0)
     own_slice(got1_ref, 0, 0).start()
     own_slice(got1_ref, 1, 0).start()
+
+    spread = row - iota((GROUP, GROUP), 1).astype(F32)
+    for h in range(heads):
+        r = rate_ref[h]
+        dec_ref[h] = jnp.where(spread >= 0.0, jnp.exp(-r * jnp.maximum(spread, 0.0)), 0.0)
+        qdec_ref[h] = jnp.exp(-r * (row + 1.0))
 
     wait_bytes(hall_ref.at[pl.ds(0, others)], hrecv)
     for d in range(devices):
@@ -249,23 +253,28 @@
 
     def scan(got_ref, half, reverse):
         def step(b, state):
-            b = total // UNROLL - 1 - b if reverse else b
-            for n in range(UNROLL):
-                t = b * UNROLL + (UNROLL - 1 - n if reverse else n)
-                hi, lo = t // HEAD, lax.rem(t, HEAD)
-                seq_ref[t] = state.astype(BF16)
-                state = carry_s[hi, lo] * state + got_ref[half][order_s[hi, lo]].astype(F32)
+            base = (total // STEPS - 1 - b if reverse else b) * STEPS
+            hi, lo = base // HEAD, lax.rem(base, HEAD)
+            arrived = [got_ref[half][order_s[hi, lo + n]] for n in range(STEPS)]
+            keeps = [carry_s[hi, lo + n] for n in range(STEPS)]
+            states = [None] * STEPS
+            for n in range(STEPS):
+                n = STEPS - 1 - n if reverse else n
+                states[n] = state.astype(BF16)
+                state = keeps[n] * state + arrived[n].astype(F32)
+            for n in range(STEPS):
+                seq_ref[base + n] = states[n]
             return state
 
-        lax.fori_loop(0, total // UNROLL, step, jnp.zeros((part, HEAD), F32))
-
-        def put(b, _):
-            for n in range(UNROLL):
-                p = b * UNROLL + n
-                back_ref[half, p] = seq_ref[homes_s[p // groups, lax.rem(p, groups)]]
+        lax.fori_loop(0, total // STEPS, step, jnp.zeros((part, HEAD), F32))
+
+        def put(d, _):
+            found = [seq_ref[homes_s[d, n]] for n in range(groups)]
+            for n in range(groups):
+                back_ref[half, d * groups + n] = found[n]
             return 0
 
-        lax.fori_loop(0, total // UNROLL, put, 0)
+        lax.fori_loop(0, devices, put, 0)
 
     half_groups = groups // 2
 
@@ -413,7 +422,7 @@
             vgp_ref[rows, cols] = dot(mix_ref[i * heads + h], g, TN)
         return 0
 
-    early = groups // 2
+    early = groups * 3 // 8
     lax.fori_loop(0, early, local_group, 0)
     sent(send2)
     turn(got2_ref, after_ref, 2, True, recv3, send4, recv4a, recv4b)

time: 111 us -> 108 us (0.973)
  Pallas kernels: 110 us -> 107 us
    pallas_call x1, Pallas kernels: 107 us -> 104 us  [shards(): pl.pallas_call(functools.partial(fused_kernel, heads, groups, devices, si...]
where the time goes in v5:
time: 108 us; the launch traced here: 107 us
  Pallas kernels  107 us (99%)
    pallas_call x1, Pallas kernels, shards(): pl.pallas_call(functools.partial(fused_kernel, heads, groups, devices, si...  104 us
    pallas_call x1, Pallas kernels, shards(): pl.pallas_call(store_kernel, out_shape=(jax.ShapeDtypeStruct((rows, width...  2.73 us

profile of v5, /device:TPU:0, one launch (start us, length us, event | category | flops | bytes accessed | tf_op | source)
XLA Modules:
  0.0 107.4 jit_solution(5136837113599429729)
XLA Ops:
  0.6 104.1 %shard_map.103 = (bf16[2048,512]{1,0:T(8,128)(2,1)S(1)}, bf16[2048,512]{1,0:T(8,128)(2,1)S(1)}, bf16[2048,512]{1,0:T(8,128)(2,1)S(1)}) custom-call(f32[4]{0:T(128)} %rate_hbm.1, s32[32]{0:T(128)} %len_hbm.1, s32[16]{0:T(128)} %home_hbm.1, f32[1,512]{1,0:T(1,128)} %bitcast.1, bf16[2048,512]{1,0:T(8,128)(2,1)} %q_hbm.1, bf16[2048,512]{1,0:T(8,128)(2,1)} %k_hbm.1, ...), custom_call_target="tpu_custom_call" | custom-call | tf_op jit(solution)/shard_map/pallas_call | solution.py:495
  104.7 2.7 %shard_map.104 = (bf16[2048,512]{1,0:T(8,128)(2,1)}, bf16[2048,512]{1,0:T(8,128)(2,1)}, bf16[2048,512]{1,0:T(8,128)(2,1)}) custom-call(bf16[2048,512]{1,0:T(8,128)(2,1)S(1)} %get-tuple-element.6.a_ref, bf16[2048,512]{1,0:T(8,128)(2,1)S(1)} %get-tuple-element.7.b_ref, bf16[2048,512]{1,0:T(8,128)(2,1)S(1)} %get-tuple-element.8.c_ref), custom_call_target="tpu_custom_call" | custom-call | tf_op jit(solution)/shard_map/pallas_call | solution.py:505

commit v6 on v5

--- a/solution.py
+++ b/solution.py
@@ -136,10 +136,6 @@
     carry_copy = pltpu.make_async_copy(carry_ref, carry_s, smem_sem.at[0])
     carry_copy.start()
 
-    pl.semaphore_wait(barrier, others + sides - 1)
-    load_q.start()
-    load_u.start()
-
     def rows_of(i):
         return pl.ds(pl.multiple_of(i * GROUP, GROUP), GROUP)
 
@@ -188,14 +184,21 @@
             store_state(i, h, dot(k_ref[rows, cols], w, TN))
         return 0
 
-    def summary_chunk(c, _):
+    def summarize(c):
         slab_copy(k_hbm, k_ref, c, kv_sem.at[0, c]).wait()
         slab_copy(v_hbm, v_ref, c, kv_sem.at[1, c]).wait()
         lax.fori_loop(c * CHUNK, (c + 1) * CHUNK, summary_group, 0)
+
+    def summary_chunk(c, _):
+        summarize(c)
         scatter(got1_ref, 0, c, send1, recv1)
         return 0
 
-    summary_chunk(0, 0)
+    summarize(0)
+    load_q.start()
+    load_u.start()
+    pl.semaphore_wait(barrier, others + sides - 1)
+    scatter(got1_ref, 0, 0, send1, recv1)
     for peer in peers:
         pltpu.make_async_remote_copy(
             src_ref=hmine_ref, dst_ref=hall_ref.at[me], send_sem=hsend, recv_sem=hrecv,

time: 108 us -> 106 us (0.981)
  no operation moved by 1% of the time
where the time goes in v6:
time: 106 us
  Pallas kernels  106 us (100%)
    pallas_call x1, Pallas kernels, shards(): pl.pallas_call(functools.partial(fused_kernel, heads, groups, devices, si...  103 us
    pallas_call x1, Pallas kernels, shards(): pl.pallas_call(store_kernel, out_shape=(jax.ShapeDtypeStruct((rows, width...  2.73 us

profile of v6, /device:TPU:0, one launch (start us, length us, event | category | flops | bytes accessed | tf_op | source)
XLA Modules:
  0.0 106.3 jit_solution(15222328251268003813)
XLA Ops:
  0.6 103.0 %shard_map.103 = (bf16[2048,512]{1,0:T(8,128)(2,1)S(1)}, bf16[2048,512]{1,0:T(8,128)(2,1)S(1)}, bf16[2048,512]{1,0:T(8,128)(2,1)S(1)}) custom-call(f32[4]{0:T(128)} %rate_hbm.1, s32[32]{0:T(128)} %len_hbm.1, s32[16]{0:T(128)} %home_hbm.1, f32[1,512]{1,0:T(1,128)} %bitcast.1, bf16[2048,512]{1,0:T(8,128)(2,1)} %q_hbm.1, bf16[2048,512]{1,0:T(8,128)(2,1)} %k_hbm.1, ...), custom_call_target="tpu_custom_call" | custom-call | tf_op jit(solution)/shard_map/pallas_call | solution.py:498
  103.6 2.7 %shard_map.104 = (bf16[2048,512]{1,0:T(8,128)(2,1)}, bf16[2048,512]{1,0:T(8,128)(2,1)}, bf16[2048,512]{1,0:T(8,128)(2,1)}) custom-call(bf16[2048,512]{1,0:T(8,128)(2,1)S(1)} %get-tuple-element.6.a_ref, bf16[2048,512]{1,0:T(8,128)(2,1)S(1)} %get-tuple-element.7.b_ref, bf16[2048,512]{1,0:T(8,128)(2,1)S(1)} %get-tuple-element.8.c_ref), custom_call_target="tpu_custom_call" | custom-call | tf_op jit(solution)/shard_map/pallas_call | solution.py:508

commit v7 on v6

--- a/solution.py
+++ b/solution.py
@@ -194,11 +194,26 @@
         scatter(got1_ref, 0, c, send1, recv1)
         return 0
 
-    summarize(0)
+    slab_copy(k_hbm, k_ref, 0, kv_sem.at[0, 0]).wait()
+    slab_copy(v_hbm, v_ref, 0, kv_sem.at[1, 0]).wait()
+    first = CHUNK // 2
+    lax.fori_loop(0, first, summary_group, 0)
+    pl.semaphore_wait(barrier, others + sides - 1)
+
+    def first_piece(n, _):
+        for peer in peers:
+            pltpu.make_async_remote_copy(
+                src_ref=send_ref.at[0, peer, pl.ds(n * first, first)],
+                dst_ref=got1_ref[0].at[pl.ds(me * groups + n * first, first)],
+                send_sem=send1, recv_sem=recv1.at[0],
+                device_id=(peer, side), device_id_type=MESH,
+            ).start()
+        lax.fori_loop((n + 1) * first, (n + 2) * first * (1 - n), summary_group, 0)
+        return 0
+
+    lax.fori_loop(0, 2, first_piece, 0)
     load_q.start()
     load_u.start()
-    pl.semaphore_wait(barrier, others + sides - 1)
-    scatter(got1_ref, 0, 0, send1, recv1)
     for peer in peers:
         pltpu.make_async_remote_copy(
             src_ref=hmine_ref, dst_ref=hall_ref.at[me], send_sem=hsend, recv_sem=hrecv,
@@ -280,6 +295,7 @@
         lax.fori_loop(0, devices, put, 0)
 
     half_groups = groups // 2
+    piece = CHUNK // 2
 
     def turn(got_ref, dst_ref, n, reverse, recv_sem, send_back, recv_first, recv_second):
         own_slice(got_ref, 0, n).wait()
@@ -300,7 +316,9 @@
             give_back(dst_ref, 1, c * CHUNK, CHUNK, send_back, recv_second.at[c])
             return 0
 
-        lax.fori_loop(0, chunks, rest, 0)
+        lax.fori_loop(0, chunks - 1, rest, 0)
+        for n in range(2):
+            give_back(dst_ref, 1, groups - CHUNK + n * piece, piece, send_back, recv_second.at[chunks - 1 + n])
 
     def turned(dst_ref, c, recv_first, recv_second):
         @pl.when(lax.rem(c, chunks // 2) == 0)
@@ -309,7 +327,12 @@
                 dst_ref.at[0, pl.ds(0, others), pl.ds(0, half_groups)], recv_first.at[c // (chunks // 2)]
             )
 
-        wait_bytes(dst_ref.at[1, pl.ds(0, others), pl.ds(0, CHUNK)], recv_second.at[c])
+        @pl.when(c < chunks - 1)
+        def _():
+            wait_bytes(dst_ref.at[1, pl.ds(0, others), pl.ds(0, CHUNK)], recv_second.at[c])
+
+    def turned_piece(dst_ref, n, recv_second):
+        wait_bytes(dst_ref.at[1, pl.ds(0, others), pl.ds(0, piece)], recv_second.at[chunks - 1 + n])
 
     def sent(sem):
         wait_bytes(send_ref.at[0, pl.ds(0, others)], sem)
@@ -350,6 +373,12 @@
 
     def output_chunk(c):
         turned(prev_ref, c, recv2a, recv2b)
+
+        @pl.when(c == chunks - 1)
+        def _():
+            turned_piece(prev_ref, 0, recv2b)
+            turned_piece(prev_ref, 1, recv2b)
+
         acc = lax.fori_loop(0, CHUNK, functools.partial(output_group, c), jnp.zeros((GROUP, HEAD), F32))
         packed = acc[0:width]
         for n in range(1, pieces):
@@ -449,7 +478,11 @@
         lax.fori_loop(c * CHUNK, (c + 1) * CHUNK, final_group, 0)
         return 0
 
-    lax.fori_loop(0, chunks, final_chunk, 0)
+    lax.fori_loop(0, chunks - 1, final_chunk, 0)
+    for n in range(2):
+        turned_piece(after_ref, n, recv4b)
+        start = groups - CHUNK + n * piece
+        lax.fori_loop(start, start + piece, final_group, 0)
     sent(send3)
     sent(send4)
 
@@ -492,7 +525,7 @@
         + [pltpu.SMEM((devices, HEAD), I32), pltpu.SMEM((8, HEAD), I32), pltpu.SMEM((8, HEAD), F32)]
         + [vmem((chunks, 2 * CHUNK, HEAD), F32), vmem((chunks, sides - 1, 2 * CHUNK, HEAD), F32)]
         + [dma((2, chunks)), dma((2,)), dma((4, 2)), dma((3,)), dma, dma]
-        + [dma, dma((2,)), dma, dma((2,)), dma((chunks,))] * 2
+        + [dma, dma((2,)), dma, dma((2,)), dma((chunks + 1,))] * 2
         + [dma((chunks,)), dma((chunks,))]
     )
     grads = pl.pallas_call(

time: 106 us -> 106 us (level)
  no operation moved by 1% of the time
where the time goes in v7:
time: 106 us
  Pallas kernels  105 us (99%)
    pallas_call x1, Pallas kernels, shards(): pl.pallas_call(functools.partial(fused_kernel, heads, groups, devices, si...  103 us
    pallas_call x1, Pallas kernels, shards(): pl.pallas_call(store_kernel, out_shape=(jax.ShapeDtypeStruct((rows, width...  2.73 us

profile of v7, /device:TPU:0, one launch (start us, length us, event | category | flops | bytes accessed | tf_op | source)
XLA Modules:
  0.0 105.9 jit_solution(11735967085350495967)
XLA Ops:
  0.6 102.6 %shard_map.103 = (bf16[2048,512]{1,0:T(8,128)(2,1)S(1)}, bf16[2048,512]{1,0:T(8,128)(2,1)S(1)}, bf16[2048,512]{1,0:T(8,128)(2,1)S(1)}) custom-call(f32[4]{0:T(128)} %rate_hbm.1, s32[32]{0:T(128)} %len_hbm.1, s32[16]{0:T(128)} %home_hbm.1, f32[1,512]{1,0:T(1,128)} %bitcast.1, bf16[2048,512]{1,0:T(8,128)(2,1)} %q_hbm.1, bf16[2048,512]{1,0:T(8,128)(2,1)} %k_hbm.1, ...), custom_call_target="tpu_custom_call" | custom-call | tf_op jit(solution)/shard_map/pallas_call | solution.py:531
  103.2 2.7 %shard_map.104 = (bf16[2048,512]{1,0:T(8,128)(2,1)}, bf16[2048,512]{1,0:T(8,128)(2,1)}, bf16[2048,512]{1,0:T(8,128)(2,1)}) custom-call(bf16[2048,512]{1,0:T(8,128)(2,1)S(1)} %get-tuple-element.6.a_ref, bf16[2048,512]{1,0:T(8,128)(2,1)S(1)} %get-tuple-element.7.b_ref, bf16[2048,512]{1,0:T(8,128)(2,1)S(1)} %get-tuple-element.8.c_ref), custom_call_target="tpu_custom_call" | custom-call | tf_op jit(solution)/shard_map/pallas_call | solution.py:541

commit v8 on v7

--- a/solution.py
+++ b/solution.py
@@ -60,7 +60,10 @@
     me = lax.axis_index("seq")
     side = lax.axis_index("head")
     y, z = me // RING, lax.rem(me, RING)
-    peers = [lax.rem(y + dy, RING) * RING + lax.rem(z + dz, RING) for dy, dz in torus_offsets(RING)]
+    flip = 1 + 2 * lax.rem(side, 2)
+    peers = [
+        lax.rem(y + dy * flip, RING) * RING + lax.rem(z + dz * flip, RING) for dy, dz in torus_offsets(RING)
+    ]
     mates = [lax.rem(side + n, sides) for n in range(1, sides)]
     got1_ref, got2_ref = (got1a_ref, got1b_ref), (got2a_ref, got2b_ref)
     others = devices - 1

time: 106 us -> 106 us (level)
  no operation moved by 1% of the time
where the time goes in v8:
time: 106 us
  Pallas kernels  105 us (99%)
    pallas_call x1, Pallas kernels, shards(): pl.pallas_call(functools.partial(fused_kernel, heads, groups, devices, si...  103 us
    pallas_call x1, Pallas kernels, shards(): pl.pallas_call(store_kernel, out_shape=(jax.ShapeDtypeStruct((rows, width...  2.73 us

profile of v8, /device:TPU:0, one launch (start us, length us, event | category | flops | bytes accessed | tf_op | source)
XLA Modules:
  0.0 105.9 jit_solution(11828612438570600254)
XLA Ops:
  0.6 102.6 %shard_map.103 = (bf16[2048,512]{1,0:T(8,128)(2,1)S(1)}, bf16[2048,512]{1,0:T(8,128)(2,1)S(1)}, bf16[2048,512]{1,0:T(8,128)(2,1)S(1)}) custom-call(f32[4]{0:T(128)} %rate_hbm.1, s32[32]{0:T(128)} %len_hbm.1, s32[16]{0:T(128)} %home_hbm.1, f32[1,512]{1,0:T(1,128)} %bitcast.1, bf16[2048,512]{1,0:T(8,128)(2,1)} %q_hbm.1, bf16[2048,512]{1,0:T(8,128)(2,1)} %k_hbm.1, ...), custom_call_target="tpu_custom_call" | custom-call | tf_op jit(solution)/shard_map/pallas_call | solution.py:534
  103.2 2.7 %shard_map.104 = (bf16[2048,512]{1,0:T(8,128)(2,1)}, bf16[2048,512]{1,0:T(8,128)(2,1)}, bf16[2048,512]{1,0:T(8,128)(2,1)}) custom-call(bf16[2048,512]{1,0:T(8,128)(2,1)S(1)} %get-tuple-element.6.a_ref, bf16[2048,512]{1,0:T(8,128)(2,1)S(1)} %get-tuple-element.7.b_ref, bf16[2048,512]{1,0:T(8,128)(2,1)S(1)} %get-tuple-element.8.c_ref), custom_call_target="tpu_custom_call" | custom-call | tf_op jit(solution)/shard_map/pallas_call | solution.py:544
